TPU v7x, 32 devices: a whole 2x2x4 slice. The times are simulated.
32 devices in a mesh: sky: 4 (over y, x), exp: 8 (over z, core).
Axes of the slice: x: 2, y: 2, z: 4, core: 2. Of those that a mesh axis runs over, the one named last changes fastest.
Arguments:
- obs_weight: float32 [4, 8, 8, 1024], P('sky', 'exp'), may hold values from 0.25 to 4
- magnitude: float32 [4, 8, 8, 1024], P('sky', 'exp'), may hold values from -18 to 18
- star_id: int32 [4, 8, 8, 1024], P('sky', 'exp'), may hold values from 0 to 4095
- peer_count: int32 [4, 8, 8], P('sky', 'exp'), may hold values from 1 to 1024, 6144 in all within a row
- zp_index: int32 [4, 8, 8, 1024], P('sky', 'exp'), may hold values from 0 to 12095
Outputs:
- zero_points: float32 [96768], P('exp')
- residual: float32 [96768], P('exp')
Inputs may be any that keep to these rules, and one draw needn't show every extreme that they name: `peer_count`: each device's counts over the 8 owners sum to 6144, and one of them equals 1024.
All inputs are finite; a program needn't handle non-finite values.
Results may differ from a plain program's by a relative error of at most 0.0003.
Values sent between devices are 32-bit elements; how exact they have to be, the bound alone decides.
No kernel may reach another device: no remote copies, remote signals or barrier semaphores. Data moves between devices by JAX's collectives and lax.ppermute only.
A program may use at most 64 MiB of HBM per device.

v0:
```python
import math

import jax
import jax.numpy as jnp
from jax import lax
from jax.sharding import PartitionSpec as P

CAP = 1024
STAR_DEV = 4096
ITERS = 2
ZP_DEV = 12096


ridge = 1.0
prior = 1.0
exact = lax.Precision.HIGHEST


def hot_parts(index, size):
    rows = (size + 127) // 128
    high = (index[:, None] // 128 == jnp.arange(rows, dtype=jnp.int32)[None, :]).astype(jnp.float32)
    low = (index[:, None] % 128 == jnp.arange(128, dtype=jnp.int32)[None, :]).astype(jnp.float32)
    return (high, low)


def sum_by(values, index, size):
    total = values.shape[0]
    block = math.gcd(total, 2048)
    count = total // block

    def sum_one_block(pair):
        high, low = hot_parts(pair[1], size)
        return jnp.einsum("sh,sl->hl", high, low * pair[0][:, None], precision=exact)

    parts = lax.map(sum_one_block, (values.reshape(count, block), index.reshape(count, block)))
    return jnp.sum(parts, axis=0).reshape(-1)[:size]


def take_by(field, index):
    size = field.shape[0]
    rows = (size + 127) // 128
    table = jnp.pad(field, (0, rows * 128 - size)).reshape(rows, 128)
    total = index.shape[0]
    block = math.gcd(total, 2048)
    count = total // block

    def take_one_block(piece):
        high, low = hot_parts(piece, size)
        picked = jnp.dot(high, table, precision=exact)
        return jnp.sum(picked * low, axis=1)

    return lax.map(take_one_block, index.reshape(count, block)).reshape(-1)


def body(obs_weight, magnitude, star_id, peer_count, zp_index):
    n_exp = lax.axis_size("exp")
    slots = jnp.arange(CAP, dtype=jnp.int32)
    live = (slots[None, :] < peer_count[0, 0][:, None]).astype(jnp.float32)
    weight = (obs_weight[0, 0] * live).reshape(-1)
    stars = star_id[0, 0].reshape(-1)
    wsum = prior + sum_by(weight, stars, STAR_DEV)
    owned = zp_index[0, 0]
    owned_flat = owned.reshape(-1)

    def reduce_slots(values):
        flat = values.reshape(-1)
        mean = sum_by(weight * flat, stars, STAR_DEV) / wsum
        term = (weight * (flat - take_by(mean, stars))).reshape(n_exp, CAP)
        arrived = lax.all_to_all(term, "exp", split_axis=0, concat_axis=0, tiled=True)
        partial_sum = sum_by(arrived.reshape(-1), owned_flat, ZP_DEV)
        return lax.psum(partial_sum, "sky")

    def slot_values(field):
        picked = take_by(field, owned_flat).reshape(n_exp, CAP)
        return lax.all_to_all(picked, "exp", split_axis=0, concat_axis=0, tiled=True)

    def operate(field):
        return reduce_slots(slot_values(field)) + ridge * field

    right = reduce_slots(magnitude[0, 0])
    zero_points = jnp.zeros_like(right)
    residual = right

    def paired(vector, image):
        return lax.psum((jnp.sum(vector * vector), jnp.sum(vector * image)), "exp")

    image = operate(residual)
    norm_now, product = paired(residual, image)
    alpha = norm_now / product
    direction = residual
    along = image
    for step in range(ITERS):
        zero_points = zero_points + alpha * direction
        residual = residual - alpha * along
        if step + 1 < ITERS:
            image = operate(residual)
            norm_next, product = paired(residual, image)
            ratio = norm_next / norm_now
            alpha = norm_next / (product - ratio * norm_next / alpha)
            direction = residual + ratio * direction
            along = image + ratio * along
            norm_now = norm_next
    return (zero_points, residual)


def solution(mesh):
    return jax.shard_map(
        body,
        mesh=mesh,
        in_specs=(
            P("sky", "exp", None, None),
            P("sky", "exp", None, None),
            P("sky", "exp", None, None),
            P("sky", "exp", None),
            P("sky", "exp", None, None),
        ),
        out_specs=(P("exp"), P("exp")),
        check_vma=False,
    )
```

profile of v0, /device:TPU:0, one launch (start us, length us, event | category | flops | bytes accessed | tf_op | source)
XLA Modules:
  0.0 222.0 jit_solution(16200304544047212028)
XLA Ops:
  4.5 7.7 %while.145 = (s32[]{:T(128)}, f32[4,32,128]{2,1,0:T(8,128)S(1)}, s32[4,2048]{1,0:T(4,128)S(1)}, f32[4,2048]{1,0:T(4,128)S(1)}, s32[]{:T(128)}) while((s32[]{:T(128)}, f32[4,32,128]{2,1,0:T(8,128)S(1)}, s32[4,2048]{1,0:T(4,128)S(1)}, f32[4,2048]{1,0:T(4,128)S(1)}, s32[]{:T(128)}) %tuple.305), condition=%wide.region_4.5_spmd, body=%wide.region_3.4_spmd.sunk | while | flops 101292032 | bytes 98377 | solution.py:35
  12.2 7.7 %while.144 = (s32[]{:T(128)}, f32[4,32,128]{2,1,0:T(8,128)S(1)}, s32[4,2048]{1,0:T(4,128)S(1)}, f32[4,2048]{1,0:T(4,128)S(1)}, s32[]{:T(128)}) while((s32[]{:T(128)}, f32[4,32,128]{2,1,0:T(8,128)S(1)}, s32[4,2048]{1,0:T(4,128)S(1)}, f32[4,2048]{1,0:T(4,128)S(1)}, s32[]{:T(128)}) %tuple.338), condition=%wide.region_1.2_spmd, body=%wide.region_0.1_spmd.sunk | while | flops 101292032 | bytes 98377 | solution.py:35
  20.0 5.4 %while.146 = (s32[]{:T(128)}, f32[4,2048]{1,0:T(4,128)S(1)}, s32[4,2048]{1,0:T(4,128)S(1)}, f32[32,128]{1,0:T(8,128)S(1)}, s32[]{:T(128)}, /*index=5*/s32[]{:T(128)}) while((s32[]{:T(128)}, f32[4,2048]{1,0:T(4,128)S(1)}, s32[4,2048]{1,0:T(4,128)S(1)}, f32[32,128]{1,0:T(8,128)S(1)}, s32[]{:T(128)}, /*index=5*/s32[]{:T(128)}) %tuple.339), condition=%wide.region_8.9_spmd, body=%wide.region_6.8_spmd.sunk | while | flops 101552128 | bytes 98381 | solution.py:52
  26.2 6.5 %all-to-all-start = ((f32[8,1,1024]{2,1,0:T(1,128)}), f32[8,1,1024]{2,1,0:T(1,128)S(1)}, u32[]{:S(2)}, u32[]{:S(2)}) async-start(f32[8,1,1024]{2,1,0:T(1,128)} %subtract_multiply_fusion.2), calls=%async_computation | async-start | bytes 65536 | tf_op jit(solution)/shard_map/all_to_all | solution.py:69
  32.7 5.7 %all-to-all-done = f32[8,1,1024]{2,1,0:T(1,128)S(1)} async-done(((f32[8,1,1024]{2,1,0:T(1,128)}), f32[8,1,1024]{2,1,0:T(1,128)S(1)}, u32[]{:S(2)}, u32[]{:S(2)}) %all-to-all-start) | async-done | bytes 32800 | tf_op jit(solution)/shard_map/all_to_all | solution.py:69
  38.5 7.9 %while.147 = (s32[]{:T(128)}, f32[4,95,128]{2,1,0:T(8,128)S(1)}, s32[4,2048]{1,0:T(4,128)S(1)}, f32[4,2048]{1,0:T(4,128)S(1)}, s32[]{:T(128)}) while((s32[]{:T(128)}, f32[4,95,128]{2,1,0:T(8,128)S(1)}, s32[4,2048]{1,0:T(4,128)S(1)}, f32[4,2048]{1,0:T(4,128)S(1)}, s32[]{:T(128)}) %tuple.311), condition=%wide.region_10.11_spmd, body=%wide.region_9.10_spmd.sunk | while | flops 299601920 | bytes 131145 | solution.py:35
  38.6 1.9 fusion.120
  40.6 1.9 fusion.120
  44.5 1.9 fusion.120
  46.5 16.7 %psum.49 = f32[12096]{0:T(1024)S(1)} all-reduce(f32[12096]{0:T(1024)S(1)} %bitcast.183), channel_id=1, replica_groups=mesh['sky'=4,'exp'=8] {'sky'}, use_global_device_ids=true, to_apply=%region_12.13 | all-reduce | flops 12096 | bytes 96768 | tf_op jit(solution)/shard_map/psum | solution.py:71
  63.2 5.7 %while.148 = (s32[]{:T(128)}, f32[4,2048]{1,0:T(4,128)S(1)}, s32[4,2048]{1,0:T(4,128)S(1)}, f32[95,128]{1,0:T(8,128)S(1)}, s32[]{:T(128)}, /*index=5*/s32[]{:T(128)}) while((s32[]{:T(128)}, f32[4,2048]{1,0:T(4,128)S(1)}, s32[4,2048]{1,0:T(4,128)S(1)}, f32[95,128]{1,0:T(8,128)S(1)}, s32[]{:T(128)}, /*index=5*/s32[]{:T(128)}) %tuple.344), condition=%wide.region_17.18_spmd, body=%wide.region_15.17_spmd.sunk | while | flops 299862016 | bytes 130637 | solution.py:52
  69.5 3.3 %all-to-all-start.1 = ((f32[8,1,1024]{2,1,0:T(1,128)}), f32[8,1,1024]{2,1,0:T(1,128)S(1)}, u32[]{:S(2)}, u32[]{:S(2)}) async-start(f32[8,1,1024]{2,1,0:T(1,128)} %all_to_all.25), calls=%async_computation.1 | async-start | bytes 65536 | tf_op jit(solution)/shard_map/all_to_all | solution.py:75
  72.9 5.7 %all-to-all-done.1 = f32[8,1,1024]{2,1,0:T(1,128)S(1)} async-done(((f32[8,1,1024]{2,1,0:T(1,128)}), f32[8,1,1024]{2,1,0:T(1,128)S(1)}, u32[]{:S(2)}, u32[]{:S(2)}) %all-to-all-start.1) | async-done | bytes 32800 | tf_op jit(solution)/shard_map/all_to_all | solution.py:75
  78.7 7.7 %while.149 = (s32[]{:T(128)}, f32[4,32,128]{2,1,0:T(8,128)S(1)}, s32[4,2048]{1,0:T(4,128)S(1)}, f32[4,2048]{1,0:T(4,128)S(1)}, s32[]{:T(128)}) while((s32[]{:T(128)}, f32[4,32,128]{2,1,0:T(8,128)S(1)}, s32[4,2048]{1,0:T(4,128)S(1)}, f32[4,2048]{1,0:T(4,128)S(1)}, s32[]{:T(128)}) %tuple.340), condition=%wide.region_19.20_spmd, body=%wide.region_18.19_spmd.sunk | while | flops 101292032 | bytes 98377 | solution.py:35
  86.5 5.4 %while.150 = (s32[]{:T(128)}, f32[4,2048]{1,0:T(4,128)S(1)}, s32[4,2048]{1,0:T(4,128)S(1)}, f32[32,128]{1,0:T(8,128)S(1)}, s32[]{:T(128)}, /*index=5*/s32[]{:T(128)}) while((s32[]{:T(128)}, f32[4,2048]{1,0:T(4,128)S(1)}, s32[4,2048]{1,0:T(4,128)S(1)}, f32[32,128]{1,0:T(8,128)S(1)}, s32[]{:T(128)}, /*index=5*/s32[]{:T(128)}) %tuple.341), condition=%wide.region_23.24_spmd, body=%wide.region_21.23_spmd.sunk | while | flops 101552128 | bytes 98381 | solution.py:52
  92.7 3.3 %all-to-all-start.2 = ((f32[8,1,1024]{2,1,0:T(1,128)}), f32[8,1,1024]{2,1,0:T(1,128)S(1)}, u32[]{:S(2)}, u32[]{:S(2)}) async-start(f32[8,1,1024]{2,1,0:T(1,128)} %subtract_multiply_fusion.1), calls=%async_computation.2 | async-start | bytes 65536 | tf_op jit(solution)/shard_map/all_to_all | solution.py:69
  96.1 5.7 %all-to-all-done.2 = f32[8,1,1024]{2,1,0:T(1,128)S(1)} async-done(((f32[8,1,1024]{2,1,0:T(1,128)}), f32[8,1,1024]{2,1,0:T(1,128)S(1)}, u32[]{:S(2)}, u32[]{:S(2)}) %all-to-all-start.2) | async-done | bytes 32800 | tf_op jit(solution)/shard_map/all_to_all | solution.py:69
  101.9 7.9 %while.151 = (s32[]{:T(128)}, f32[4,95,128]{2,1,0:T(8,128)S(1)}, s32[4,2048]{1,0:T(4,128)S(1)}, f32[4,2048]{1,0:T(4,128)S(1)}, s32[]{:T(128)}) while((s32[]{:T(128)}, f32[4,95,128]{2,1,0:T(8,128)S(1)}, s32[4,2048]{1,0:T(4,128)S(1)}, f32[4,2048]{1,0:T(4,128)S(1)}, s32[]{:T(128)}) %tuple.345), condition=%wide.region_25.26_spmd, body=%wide.region_24.25_spmd.sunk | while | flops 299601920 | bytes 131145 | solution.py:35
  103.9 1.9 fusion.128
  105.9 1.9 fusion.128
  107.8 1.9 fusion.128
  109.8 14.7 %psum.51 = f32[12096]{0:T(1024)S(1)} all-reduce(f32[12096]{0:T(1024)S(1)} %bitcast.184), channel_id=1, replica_groups=mesh['sky'=4,'exp'=8] {'sky'}, use_global_device_ids=true, to_apply=%region_27.28 | all-reduce | flops 12096 | bytes 96768 | tf_op jit(solution)/shard_map/psum | solution.py:71
  125.2 14.3 %all-reduce.3 = (f32[]{:T(128)}, f32[]{:T(128)}) all-reduce(f32[]{:T(128)} %get-tuple-element.689, f32[]{:T(128)} %get-tuple-element.688), channel_id=1, replica_groups=mesh['sky'=4,'exp'=8] {'exp'}, use_global_device_ids=true, to_apply=%region_14.15 | all-reduce | flops 2 | bytes 16 | tf_op jit(solution)/shard_map/psum | solution.py:85
  140.8 5.7 %while.152 = (s32[]{:T(128)}, f32[4,2048]{1,0:T(4,128)S(1)}, s32[4,2048]{1,0:T(4,128)S(1)}, f32[95,128]{1,0:T(8,128)S(1)}, s32[]{:T(128)}, /*index=5*/s32[]{:T(128)}) while((s32[]{:T(128)}, f32[4,2048]{1,0:T(4,128)S(1)}, s32[4,2048]{1,0:T(4,128)S(1)}, f32[95,128]{1,0:T(8,128)S(1)}, s32[]{:T(128)}, /*index=5*/s32[]{:T(128)}) %tuple.346), condition=%wide.region_34.35_spmd, body=%wide.region_32.34_spmd.sunk | while | flops 299862016 | bytes 130637 | solution.py:52
  147.1 3.3 %all-to-all-start.3 = ((f32[8,1,1024]{2,1,0:T(1,128)}), f32[8,1,1024]{2,1,0:T(1,128)S(1)}, u32[]{:S(2)}, u32[]{:S(2)}) async-start(f32[8,1,1024]{2,1,0:T(1,128)} %all_to_all.28), calls=%async_computation.3 | async-start | bytes 65536 | tf_op jit(solution)/shard_map/all_to_all | solution.py:75
  150.5 5.7 %all-to-all-done.3 = f32[8,1,1024]{2,1,0:T(1,128)S(1)} async-done(((f32[8,1,1024]{2,1,0:T(1,128)}), f32[8,1,1024]{2,1,0:T(1,128)S(1)}, u32[]{:S(2)}, u32[]{:S(2)}) %all-to-all-start.3) | async-done | bytes 32800 | tf_op jit(solution)/shard_map/all_to_all | solution.py:75
  156.3 7.7 %while.153 = (s32[]{:T(128)}, f32[4,32,128]{2,1,0:T(8,128)S(1)}, s32[4,2048]{1,0:T(4,128)S(1)}, f32[4,2048]{1,0:T(4,128)S(1)}, s32[]{:T(128)}) while((s32[]{:T(128)}, f32[4,32,128]{2,1,0:T(8,128)S(1)}, s32[4,2048]{1,0:T(4,128)S(1)}, f32[4,2048]{1,0:T(4,128)S(1)}, s32[]{:T(128)}) %tuple.342), condition=%wide.region_36.37_spmd, body=%wide.region_35.36_spmd.sunk | while | flops 101292032 | bytes 98377 | solution.py:35
  164.1 5.4 %while.154 = (s32[]{:T(128)}, f32[4,2048]{1,0:T(4,128)S(1)}, s32[4,2048]{1,0:T(4,128)S(1)}, f32[32,128]{1,0:T(8,128)S(1)}, s32[]{:T(128)}, /*index=5*/s32[]{:T(128)}) while((s32[]{:T(128)}, f32[4,2048]{1,0:T(4,128)S(1)}, s32[4,2048]{1,0:T(4,128)S(1)}, f32[32,128]{1,0:T(8,128)S(1)}, s32[]{:T(128)}, /*index=5*/s32[]{:T(128)}) %tuple.343), condition=%wide.region_40.41_spmd, body=%wide.region_38.40_spmd.sunk | while | flops 101552128 | bytes 98381 | solution.py:52
  169.7 8.1 %all_to_all.36 = f32[8,1,1024]{2,1,0:T(1,128)S(1)} all-to-all(f32[8,1,1024]{2,1,0:T(1,128)S(1)} %subtract_multiply_fusion), channel_id=1, replica_groups=mesh['sky'=4,'exp'=8] {'exp'}, dimensions={0} | all-to-all | bytes 65536 | tf_op jit(solution)/shard_map/all_to_all | solution.py:69
  177.9 7.9 %while.155 = (s32[]{:T(128)}, f32[4,95,128]{2,1,0:T(8,128)S(1)}, s32[4,2048]{1,0:T(4,128)S(1)}, f32[4,2048]{1,0:T(4,128)S(1)}, s32[]{:T(128)}) while((s32[]{:T(128)}, f32[4,95,128]{2,1,0:T(8,128)S(1)}, s32[4,2048]{1,0:T(4,128)S(1)}, f32[4,2048]{1,0:T(4,128)S(1)}, s32[]{:T(128)}) %tuple.347), condition=%wide.region_42.43_spmd, body=%wide.region_41.42_spmd.sunk | while | flops 299601920 | bytes 131145 | solution.py:35
  185.8 16.0 %psum.54 = f32[12096]{0:T(1024)S(1)} all-reduce(f32[12096]{0:T(1024)S(1)} %bitcast.182), channel_id=1, replica_groups=mesh['sky'=4,'exp'=8] {'sky'}, use_global_device_ids=true, to_apply=%region_44.45 | all-reduce | flops 12096 | bytes 96768 | tf_op jit(solution)/shard_map/psum | solution.py:71
  202.5 14.2 %all-reduce.2 = (f32[]{:T(128)}, f32[]{:T(128)}) all-reduce(f32[]{:T(128)} %get-tuple-element.687, f32[]{:T(128)} %get-tuple-element.686), channel_id=1, replica_groups=mesh['sky'=4,'exp'=8] {'exp'}, use_global_device_ids=true, to_apply=%region_31.32 | all-reduce | flops 2 | bytes 16 | tf_op jit(solution)/shard_map/psum | solution.py:85
  (256 shorter events, 78.5 us)
Async XLA Ops:
  0.6 0.7 copy-start.4
  2.1 0.8 copy-start.1
  2.9 0.8 copy-start
  3.6 0.8 copy-start.2
  26.2 6.5 %copy-start.3 = (s32[1,1,8,1024]{3,2,1,0:T(8,128)S(1)}, s32[1,1,8,1024]{3,2,1,0:T(8,128)}, u32[]{:S(2)}) copy-start(s32[1,1,8,1024]{3,2,1,0:T(8,128)} %param.33) | copy-start | bytes 98308
  26.2 12.2 %all-to-all-start = ((f32[8,1,1024]{2,1,0:T(1,128)}), f32[8,1,1024]{2,1,0:T(1,128)S(1)}, u32[]{:S(2)}, u32[]{:S(2)}) async-start(f32[8,1,1024]{2,1,0:T(1,128)} %subtract_multiply_fusion.2), calls=%async_computation | async-start | bytes 65536 | tf_op jit(solution)/shard_map/all_to_all | solution.py:69
  69.5 9.0 %all-to-all-start.1 = ((f32[8,1,1024]{2,1,0:T(1,128)}), f32[8,1,1024]{2,1,0:T(1,128)S(1)}, u32[]{:S(2)}, u32[]{:S(2)}) async-start(f32[8,1,1024]{2,1,0:T(1,128)} %all_to_all.25), calls=%async_computation.1 | async-start | bytes 65536 | tf_op jit(solution)/shard_map/all_to_all | solution.py:75
  92.7 9.0 %all-to-all-start.2 = ((f32[8,1,1024]{2,1,0:T(1,128)}), f32[8,1,1024]{2,1,0:T(1,128)S(1)}, u32[]{:S(2)}, u32[]{:S(2)}) async-start(f32[8,1,1024]{2,1,0:T(1,128)} %subtract_multiply_fusion.1), calls=%async_computation.2 | async-start | bytes 65536 | tf_op jit(solution)/shard_map/all_to_all | solution.py:69
  147.1 9.0 %all-to-all-start.3 = ((f32[8,1,1024]{2,1,0:T(1,128)}), f32[8,1,1024]{2,1,0:T(1,128)S(1)}, u32[]{:S(2)}, u32[]{:S(2)}) async-start(f32[8,1,1024]{2,1,0:T(1,128)} %all_to_all.28), calls=%async_computation.3 | async-start | bytes 65536 | tf_op jit(solution)/shard_map/all_to_all | solution.py:75
where the time goes:
time: 223 us; the launch traced here: 222 us
  blocking collectives  84.1 us (38%)
  matrix products  76 us (34%)
  waiting for transfers between devices  22.7 us (10%)
  starting transfers between devices  16.5 us (7%)
  local copies, waits for them, and re-layouts  8.41 us (4%)
  between operations  7 us (3%)
  other arithmetic  5.33 us (2%)
    dot_general x28, matrix products, sum_one_block(): jnp.einsum('sh,sl->hl', high, low * pair[0][:, None], precision=exact)  52.4 us
    psum x3, blocking collectives, reduce_slots(): return lax.psum(partial_sum, 'sky')  47.4 us
    psum x2, blocking collectives, paired(): return lax.psum((jnp.sum(vector * vector), jnp.sum(vector * image)), 'exp')  28.5 us
    dot_general x20, matrix products, take_one_block(): picked = jnp.dot(high, table, precision=exact)  23.7 us
    all_to_all x2, waiting for transfers between devices, reduce_slots(): lax.all_to_all(term, 'exp', split_axis=0, concat_axis=0, tiled=True)  11.4 us
    all_to_all x2, waiting for transfers between devices, slot_values(): lax.all_to_all(picked, 'exp', split_axis=0, concat_axis=0, tiled=True)  11.3 us
    all_to_all x2, starting transfers between devices, reduce_slots(): lax.all_to_all(term, 'exp', split_axis=0, concat_axis=0, tiled=True)  9.8 us
    all_to_all x1, blocking collectives, reduce_slots(): lax.all_to_all(term, 'exp', split_axis=0, concat_axis=0, tiled=True)  8.12 us
  transfers between devices with their start and end apart: 4, of which 4 were waited for; matrix products, arithmetic and copies ran while one was open for 0% of the time, Pallas kernels for 0%

commit v1 on v0

v1 whole, which is shorter than its diff:
```python
import functools

import jax
import jax.numpy as jnp
from jax import lax
from jax.experimental import pallas as pl
from jax.experimental.pallas import tpu as pltpu
from jax.sharding import PartitionSpec as P

STAR_DEV = 4096
ZP_DEV = 12096
LANES = 128
SUB = 8
ridge = 1.0
prior = 1.0

f32 = jnp.float32
bf16 = jnp.bfloat16
i16 = jnp.int16
STAR_ROWS = STAR_DEV // LANES
ZP_ROWS = -(-ZP_DEV // (LANES * 16)) * 16
CONTRACT_LANES = (((1,), (1,)), ((), ()))


def hot_rows(index, values, rows):
    position = lax.broadcasted_iota(i16, (16, LANES), 0)
    high = jnp.broadcast_to(index >> 7, (16, LANES)).astype(i16)
    low = jnp.broadcast_to(index & 127, (16, LANES)).astype(i16)
    one, zero = jnp.ones((), bf16), jnp.zeros((), bf16)
    masks = [position + jnp.int16(16 * step) == high for step in range(rows // 16)]
    upper = []
    for value in values:
        spread = jnp.broadcast_to(value, (16, LANES)).astype(bf16)
        upper.extend(jnp.where(mask, spread, zero) for mask in masks)
    lower = [jnp.where(position + jnp.int16(16 * step) == low, one, zero) for step in range(LANES // 16)]
    return jnp.concatenate(upper, 0), jnp.concatenate(lower, 0)


def halves(value):
    top = value.astype(bf16).astype(f32)
    return [top, value - top]


def sum_rows(pairs, rows):
    uppers, lowers = [], []
    for index, values in pairs:
        parts = [part for value in values for part in halves(value)]
        upper, lower = hot_rows(index, parts, rows)
        uppers.append(upper)
        lowers.append(lower)
    total = lax.dot_general(jnp.concatenate(uppers, 1), jnp.concatenate(lowers, 1), CONTRACT_LANES, preferred_element_type=f32)
    return [total[2 * n * rows:(2 * n + 1) * rows] + total[(2 * n + 1) * rows:(2 * n + 2) * rows] for n in range(len(pairs[0][1]))]


def pick(table_ref, index, rows):
    high, low = index >> 7, index & 127
    found = jnp.zeros((SUB, LANES), f32)
    for row in range(rows):
        line = jnp.broadcast_to(table_ref[row:row + 1, :], (SUB, LANES))
        found = jnp.where(high == row, jnp.take_along_axis(line, low, axis=1), found)
    return found


def tiles(n_rows, cap):
    return [(g, a) for g in range(n_rows // SUB) for a in range(cap // LANES)]


def at(g, a):
    return (pl.ds(g * SUB, SUB), pl.ds(a * LANES, LANES))


def lane_row(ref, r, a):
    return ref[r:r + 1, a * LANES:(a + 1) * LANES]


def whole_sum(x):
    return jnp.sum(jnp.sum(x, axis=1, keepdims=True), axis=0, keepdims=True)


def star_sums(star_ref, value_refs, n_rows, cap, sums_refs):
    for ref in sums_refs:
        ref[...] = jnp.zeros_like(ref)

    def block(g, carry):
        stars = star_ref[pl.ds(pl.multiple_of(g * SUB, SUB), SUB), :]
        values = [ref[pl.ds(pl.multiple_of(g * SUB, SUB), SUB), :] for ref in value_refs]
        pairs = []
        for r in range(SUB):
            for a in range(cap // LANES):
                cut = (slice(r, r + 1), slice(a * LANES, (a + 1) * LANES))
                pairs.append((stars[cut], [value[cut] for value in values]))
        for ref, part in zip(sums_refs, sum_rows(pairs, STAR_ROWS)):
            ref[...] += part
        return carry

    lax.fori_loop(0, n_rows // SUB, block, 0)


def first_terms(n_sky, count_ref, weight_ref, magnitude_ref, star_ref, terms_ref, live_ref, scale_ref, moment_ref, sums_ref, mean_ref):
    n_rows, cap = weight_ref.shape[2:]
    sub = lax.broadcasted_iota(jnp.int32, (SUB, LANES), 0)
    lane = lax.broadcasted_iota(jnp.int32, (SUB, LANES), 1)
    for g in range(n_rows // SUB):
        count = jnp.zeros((SUB, LANES), jnp.int32)
        for r in range(SUB):
            count = jnp.where(sub == r, count_ref[0, 0, g * SUB + r], count)
        for a in range(cap // LANES):
            where = at(g, a)
            live = jnp.where(lane + a * LANES < count, weight_ref[(0, 0) + where], 0.0)
            live_ref[where] = live
            moment_ref[where] = live * magnitude_ref[(0, 0) + where]
    star_sums(star_ref.at[0, 0], [live_ref, moment_ref], n_rows, cap, [scale_ref, sums_ref])
    scale_ref[...] = 1.0 / (prior + scale_ref[...])
    mean_ref[...] = sums_ref[...] * scale_ref[...]
    for g in range(n_rows // SUB):
        for a in range(cap // LANES):
            where = at(g, a)
            mean = pick(mean_ref, star_ref[(0, 0) + where], STAR_ROWS)
            term = live_ref[where] * (magnitude_ref[(0, 0) + where] - mean)
            for i in range(n_sky):
                terms_ref[i * n_rows + g * SUB:i * n_rows + (g + 1) * SUB, a, :] = term


def owner_sums(zp_ref, arrived, n_groups, cap, total_ref):
    total_ref[...] = jnp.zeros_like(total_ref)

    def block(g, carry):
        index = zp_ref[pl.ds(pl.multiple_of(g * SUB, SUB), SUB), :]
        pairs = []
        for r in range(SUB):
            for a in range(cap // LANES):
                pairs.append((index[r:r + 1, a * LANES:(a + 1) * LANES], [arrived(g, r, a)]))
        total_ref[...] += sum_rows(pairs, ZP_ROWS)[0]
        return carry

    lax.fori_loop(0, n_groups, block, 0)


def send_picks(zp_ref, table_ref, out_ref, scalar):
    n_rows, cap = zp_ref.shape[2:]
    for g in range(n_rows // SUB):

        def one(a, carry, g=g):
            lanes = pl.ds(pl.multiple_of(a * LANES, LANES), LANES)
            index = zp_ref[0, 0, g * SUB:(g + 1) * SUB, lanes]
            out_ref[g * SUB:(g + 1) * SUB, pl.ds(a, 1), :] = pick(table_ref, index, ZP_ROWS).reshape(SUB, 1, LANES)
            return carry

        lax.fori_loop(0, cap // LANES, one, 0, unroll=2)
    out_ref[:, cap // LANES, :] = jnp.broadcast_to(scalar, (n_rows, LANES))


def first_owner(n_sky, me_ref, arrived_ref, *refs):
    zp_refs, (sent_ref, all_ref, right_ref) = refs[:n_sky], refs[n_sky:]
    n_rows, cap = zp_refs[0].shape[2:]
    for d in range(n_sky):
        start = pl.multiple_of((me_ref[0] ^ d) * n_rows, SUB)
        all_ref[pl.ds(start, n_rows), :] = zp_refs[d][0, 0]

    def arrived(g, r, a):
        return arrived_ref[pl.ds(g * SUB + r, 1), a, :]

    owner_sums(all_ref, arrived, n_sky * n_rows // SUB, cap, right_ref)
    right = right_ref[...]
    send_picks(zp_refs[0], right_ref, sent_ref, whole_sum(right * right))


def star_terms(n_sky, star_ref, live_ref, scale_ref, slot_ref, product_ref, sums_ref, mean_ref, emit):
    n_rows, cap = live_ref.shape
    for g, a in tiles(n_rows, cap):
        product_ref[at(g, a)] = live_ref[at(g, a)] * slot_ref[at(g, a)]
    star_sums(star_ref.at[0, 0], [product_ref], n_rows, cap, [sums_ref])
    mean_ref[...] = sums_ref[...] * scale_ref[...]
    along = jnp.zeros((SUB, LANES), f32)
    for g, a in tiles(n_rows, cap):
        where = at(g, a)
        mean = pick(mean_ref, star_ref[(0, 0) + where], STAR_ROWS)
        slot = slot_ref[where]
        term = live_ref[where] * (slot - mean)
        along = along + slot * term
        emit(g, a, term)
    return whole_sum(along)


def second_terms(n_sky, values_ref, star_ref, live_ref, scale_ref, terms_ref, slot_ref, product_ref, sums_ref, mean_ref):
    n_rows, cap = live_ref.shape
    for g, a in tiles(n_rows, cap):
        slot_ref[at(g, a)] = values_ref[g * SUB:(g + 1) * SUB, a, :]

    def emit(g, a, term):
        for i in range(n_sky):
            terms_ref[i * n_rows + g * SUB:i * n_rows + (g + 1) * SUB, a, :] = term

    star_terms(n_sky, star_ref, live_ref, scale_ref, slot_ref, product_ref, sums_ref, mean_ref, emit)


def second_owner(arrived_ref, all_ref, right_ref, zp_ref, sent_ref, image_ref):
    n_rows, cap = zp_ref.shape[2:]

    def arrived(g, r, a):
        return arrived_ref[pl.ds(g * SUB + r, 1), a, :]

    owner_sums(all_ref, arrived, all_ref.shape[0] // SUB, cap, image_ref)
    right = right_ref[...]
    image_ref[...] = image_ref[...] + ridge * right
    send_picks(zp_ref, image_ref, sent_ref, whole_sum(right * image_ref[...]))


def third_terms(n_sky, first_ref, second_ref, star_ref, live_ref, scale_ref, right_ref, image_ref,
                terms_ref, residual_ref, scalar_ref, slot_ref, product_ref, sums_ref, mean_ref):
    n_rows, cap = live_ref.shape
    extra = cap // LANES
    norm = jnp.sum(first_ref[:, extra, :], axis=0, keepdims=True)
    product = jnp.sum(second_ref[:, extra, :], axis=0, keepdims=True)
    alpha = norm / product
    scalar_ref[0:1, :] = norm
    scalar_ref[1:2, :] = alpha
    residual = right_ref[...] - alpha * image_ref[...]
    residual_ref[...] = residual
    square = whole_sum(residual * residual)
    for g, a in tiles(n_rows, cap):
        rows = slice(g * SUB, (g + 1) * SUB)
        slot_ref[at(g, a)] = first_ref[rows, a, :] - alpha * second_ref[rows, a, :]

    def emit(g, a, term):
        for i in range(n_sky):
            terms_ref[i * n_rows + g * SUB:i * n_rows + (g + 1) * SUB, a * LANES:(a + 1) * LANES] = term

    along = star_terms(n_sky, star_ref, live_ref, scale_ref, slot_ref, product_ref, sums_ref, mean_ref, emit)
    lane = lax.broadcasted_iota(jnp.int32, (1, LANES), 1)
    both = jnp.where(lane < LANES // 2, along, square * (1.0 / n_sky))
    terms_ref[:, cap:cap + LANES] = jnp.broadcast_to(both, (n_sky * n_rows, LANES))


def last_owner(arrived_ref, all_ref, right_ref, image_ref, residual_ref, scalar_ref, points_ref, left_ref, total_ref):
    cap = all_ref.shape[1]

    def arrived(g, r, a):
        return arrived_ref[pl.ds(pl.multiple_of(g * SUB, SUB), SUB), a * LANES:(a + 1) * LANES][r:r + 1]

    owner_sums(all_ref, arrived, all_ref.shape[0] // SUB, cap, total_ref)
    sums = jnp.sum(arrived_ref[:, cap:cap + LANES], axis=0, keepdims=True)
    norm_next = sums[:, LANES // 2:LANES // 2 + 1]
    product = sums[:, 0:1] + ridge * norm_next
    norm, alpha = scalar_ref[0:1, 0:1], scalar_ref[1:2, 0:1]
    ratio = norm_next / norm
    step = norm_next / (product - ratio * norm_next / alpha)
    right, residual = right_ref[...], residual_ref[...]
    direction = residual + ratio * right
    along = (total_ref[...] + ridge * residual) + ratio * image_ref[...]
    points_ref[...] = alpha * right + step * direction
    left_ref[...] = residual - step * along


def call(kernel, shapes, scratch=(), flops=2_000_000, **more):
    return pl.pallas_call(
        kernel,
        out_shape=[jax.ShapeDtypeStruct(shape, f32) for shape in shapes],
        scratch_shapes=[pltpu.VMEM(shape, f32) for shape in scratch],
        compiler_params=pltpu.CompilerParams(vmem_limit_bytes=40 << 20),
        cost_estimate=pl.CostEstimate(flops=flops * 1000, bytes_accessed=1 << 20, transcendentals=0),
        **more,
    )


def body(obs_weight, magnitude, star_id, peer_count, zp_index):
    n_sky, n_exp = lax.axis_size("sky"), lax.axis_size("exp")
    cap = obs_weight.shape[3]
    tall, star, slots = (ZP_ROWS, LANES), (STAR_ROWS, LANES), (n_exp, cap)
    terms = (n_sky * n_exp, cap // LANES, LANES)
    picks = (n_exp, 2 * SUB, LANES)
    vmem = pl.BlockSpec(memory_space=pltpu.VMEM)
    smem = pl.BlockSpec(memory_space=pltpu.SMEM)
    me = jnp.reshape(lax.axis_index("sky"), (1,)).astype(jnp.int32)

    def to_owners(x):
        return lax.all_to_all(x, ("sky", "exp"), split_axis=0, concat_axis=0, tiled=True)

    def to_sources(x):
        return lax.all_to_all(x, "exp", split_axis=0, concat_axis=0, tiled=True)

    zp = [zp_index] + [lax.ppermute(zp_index, "sky", [(i, i ^ d) for i in range(n_sky)]) for d in range(1, n_sky)]
    sent, live, scale = call(
        functools.partial(first_terms, n_sky), [terms, slots, star], [slots, star, star],
        in_specs=[smem, vmem, vmem, vmem],
    )(peer_count, obs_weight, magnitude, star_id)
    arrived = to_owners(sent)
    sent, zp_all, right = pl.pallas_call(
        functools.partial(first_owner, n_sky),
        out_shape=[jax.ShapeDtypeStruct(picks, f32), jax.ShapeDtypeStruct((n_sky * n_exp, cap), jnp.int32), jax.ShapeDtypeStruct(tall, f32)],
        in_specs=[smem] + [vmem] * (n_sky + 1),
        compiler_params=pltpu.CompilerParams(vmem_limit_bytes=40 << 20),
    )(me, arrived, *zp)
    first = to_sources(sent)
    (sent,) = call(functools.partial(second_terms, n_sky), [terms], [slots, slots, star, star])(first, star_id, live, scale)
    arrived = to_owners(sent)
    sent, image = call(second_owner, [picks, tall])(arrived, zp_all, right, zp_index)
    second = to_sources(sent)
    sent, residual, scalars = call(
        functools.partial(third_terms, n_sky), [(n_sky * n_exp, cap + LANES), tall, (SUB, LANES)], [slots, slots, star, star]
    )(first, second, star_id, live, scale, right, image)
    arrived = to_owners(sent)
    points, left = call(last_owner, [tall, tall], [tall])(arrived, zp_all, right, image, residual, scalars)
    return points.reshape(-1)[:ZP_DEV], left.reshape(-1)[:ZP_DEV]


def solution(mesh):
    return jax.shard_map(
        body,
        mesh=mesh,
        in_specs=(
            P("sky", "exp", None, None),
            P("sky", "exp", None, None),
            P("sky", "exp", None, None),
            P("sky", "exp", None),
            P("sky", "exp", None, None),
        ),
        out_specs=(P("exp"), P("exp")),
        check_vma=False,
    )
```

time: 223 us -> 78 us (0.35)
  matrix products: 76 us -> 0 us
  blocking collectives: 84.1 us -> 37.8 us
  Pallas kernels: 0 us -> 20.3 us
  waiting for transfers between devices: 22.7 us -> 4.61 us
  between operations: 7 us -> 0.71 us
  starting transfers between devices: 16.5 us -> 10.9 us
  other arithmetic: 5.33 us -> 0 us
  local copies, waits for them, and re-layouts: 8.41 us -> 3.09 us
    dot_general x48 -> x0, matrix products: 76 us -> none  [the longest x28 52.4 us: sum_one_block(): jnp.einsum('sh,sl->hl', high, low * pair[0][:, None], precision=exact)]
    psum x5 -> x0, blocking collectives: 75.9 us -> none  [the longest x3 47.4 us: reduce_slots(): return lax.psum(partial_sum, 'sky')]
    all_to_all x1 -> x4, blocking collectives: 8.12 us -> 37.8 us  [the longest x2 20.2 us: to_owners(): lax.all_to_all(x, ('sky', 'exp'), split_axis=0, concat_axis=0, tiled=True)]
    all_to_all x4 -> x1, waiting for transfers between devices: 22.7 us -> 0.88 us  [to_owners(): lax.all_to_all(x, ('sky', 'exp'), split_axis=0, concat_axis=0, tiled=True)]
    pallas_call x0 -> x6, Pallas kernels: none -> 20.3 us  [the longest x1 5.21 us: body(): pl.pallas_call(functools.partial(first_owner, n_sky), out_shape=[jax.Shap...]
    all_to_all x4 -> x1, starting transfers between devices: 16.5 us -> 7.3 us  [to_owners(): lax.all_to_all(x, ('sky', 'exp'), split_axis=0, concat_axis=0, tiled=True)]
    ppermute x0 -> x3, waiting for transfers between devices: none -> 3.73 us  [body(): lax.ppermute(zp_index, 'sky', [(i, i ^ d) for i in range(n_sky)])]
    ppermute x0 -> x3, starting transfers between devices: none -> 3.55 us  [body(): lax.ppermute(zp_index, 'sky', [(i, i ^ d) for i in range(n_sky)])]
where the time goes in v1:
time: 78 us; the launch traced here: 77.4 us
  blocking collectives  37.8 us (48%)
  Pallas kernels  20.3 us (26%)
  starting transfers between devices  10.9 us (14%)
  waiting for transfers between devices  4.61 us (6%)
  local copies, waits for them, and re-layouts  3.09 us (4%)
    all_to_all x2, blocking collectives, to_owners(): lax.all_to_all(x, ('sky', 'exp'), split_axis=0, concat_axis=0, tiled=True)  20.2 us
    all_to_all x2, blocking collectives, to_sources(): return lax.all_to_all(x, 'exp', split_axis=0, concat_axis=0, tiled=True)  17.6 us
    all_to_all x1, starting transfers between devices, to_owners(): lax.all_to_all(x, ('sky', 'exp'), split_axis=0, concat_axis=0, tiled=True)  7.3 us
    pallas_call x1, Pallas kernels, body(): pl.pallas_call(functools.partial(first_owner, n_sky), out_shape=[jax.Shap...  5.21 us
    pallas_call x1, Pallas kernels, body(): call(second_owner, [picks, tall])(arrived, zp_all, right, zp_index)  5.2 us
    pallas_call x1, Pallas kernels, body(): call(last_owner, [tall, tall], [tall])  4.92 us
    ppermute x3, waiting for transfers between devices, body(): lax.ppermute(zp_index, 'sky', [(i, i ^ d) for i in range(n_sky)])  3.73 us
    ppermute x3, starting transfers between devices, body(): lax.ppermute(zp_index, 'sky', [(i, i ^ d) for i in range(n_sky)])  3.55 us
  transfers between devices with their start and end apart: 4, of which 4 were waited for; matrix products, arithmetic and copies ran while one was open for 0% of the time, Pallas kernels for 0%

profile of v1, /device:TPU:0, one launch (start us, length us, event | category | flops | bytes accessed | tf_op | source)
XLA Modules:
  0.0 77.4 jit_solution(8923680234881016884)
XLA Ops:
  0.6 0.0 copy-start.1
  0.6 0.7 copy-done.1
  1.4 0.0 copy-start.2
  1.4 0.8 copy-done.2
  2.1 0.0 copy-start.3
  2.1 0.8 copy-done.3
  2.9 0.0 copy-start.5
  2.9 0.7 copy-done.5
  3.6 2.3 %shard_map.68 = (f32[32,8,128]{2,1,0:T(8,128)}, f32[8,1024]{1,0:T(8,128)S(1)}, f32[32,128]{1,0:T(8,128)S(1)}) custom-call(s32[1,1,8]{2,1,0:T(1,128)S(1)} %copy-done.5, f32[1,1,8,1024]{3,2,1,0:T(8,128)S(1)} %copy-done.1, f32[1,1,8,1024]{3,2,1,0:T(8,128)S(1)} %copy-done.2, s32[1,1,8,1024]{3,2,1,0:T(8,128)S(1)} %copy-done.3), custom_call_target="tpu_custom_call" | custom-call | flops 2000000000 | bytes 1048576 | tf_op jit(solution)/shard_map/pallas_call | solution.py:283
  5.9 0.0 copy-start
  5.9 7.3 %all-to-all-start = ((f32[32,8,128]{2,1,0:T(8,128)}), f32[32,8,128]{2,1,0:T(8,128)S(1)}, u32[]{:S(2)}, u32[]{:S(2)}) async-start(f32[32,8,128]{2,1,0:T(8,128)} %get-tuple-element.15), calls=%async_computation | async-start | bytes 262144 | tf_op jit(solution)/shard_map/all_to_all | solution.py:277
  13.2 0.0 copy-done
  13.2 2.7 %collective-permute-start.2 = (s32[1,1,8,1024]{3,2,1,0:T(8,128)S(1)}, s32[1,1,8,1024]{3,2,1,0:T(8,128)S(1)}, u32[]{:S(2)}, u32[]{:S(2)}) collective-permute-start(s32[1,1,8,1024]{3,2,1,0:T(8,128)S(1)} %copy-done), channel_id=1, source_target_pairs={{0,24},{8,16},{16,8},{24,0},{1,25},{9,17},{17,9},{25,1},{2,26},{10... | collective-permute-start | bytes 98312 | tf_op jit(solution)/shard_map/ppermute | solution.py:282
  16.0 0.6 collective-permute-start.1
  16.5 0.3 collective-permute-start
  16.8 1.5 %collective-permute-done.2.refs_3_ = s32[1,1,8,1024]{3,2,1,0:T(8,128)S(1)} collective-permute-done((s32[1,1,8,1024]{3,2,1,0:T(8,128)S(1)}, s32[1,1,8,1024]{3,2,1,0:T(8,128)S(1)}, u32[]{:S(2)}, u32[]{:S(2)}) %collective-permute-start.2) | collective-permute-done | bytes 32800 | tf_op jit(solution)/shard_map/ppermute | solution.py:282
  18.3 1.8 %collective-permute-done.1.refs_2_ = s32[1,1,8,1024]{3,2,1,0:T(8,128)S(1)} collective-permute-done((s32[1,1,8,1024]{3,2,1,0:T(8,128)S(1)}, s32[1,1,8,1024]{3,2,1,0:T(8,128)S(1)}, u32[]{:S(2)}, u32[]{:S(2)}) %collective-permute-start.1) | collective-permute-done | bytes 32800 | tf_op jit(solution)/shard_map/ppermute | solution.py:282
  20.1 0.4 collective-permute-done.refs_1_
  20.5 0.9 %all-to-all-done.arrived_ref = f32[32,8,128]{2,1,0:T(8,128)S(1)} async-done(((f32[32,8,128]{2,1,0:T(8,128)}), f32[32,8,128]{2,1,0:T(8,128)S(1)}, u32[]{:S(2)}, u32[]{:S(2)}) %all-to-all-start) | async-done | bytes 131104 | tf_op jit(solution)/shard_map/all_to_all | solution.py:277
  21.4 5.2 %shard_map.69 = (f32[8,16,128]{2,1,0:T(8,128)S(1)}, s32[32,1024]{1,0:T(8,128)S(1)}, f32[96,128]{1,0:T(8,128)S(1)}) custom-call(s32[1]{0:T(128)} %bitcast.me_ref, f32[32,8,128]{2,1,0:T(8,128)S(1)} %all-to-all-done.arrived_ref, s32[1,1,8,1024]{3,2,1,0:T(8,128)S(1)} %copy-done, s32[1,1,8,1024]{3,2,1,0:T(8,128)S(1)} %collective-permute-done.refs_1_, ...), custom_call_target="tpu_custom_call" | custom-call | tf_op jit(solution)/shard_map/pallas_call | solution.py:288
  26.6 0.0 copy-start.4
  26.6 9.4 %all_to_all.31.values_ref.first_ref = f32[8,16,128]{2,1,0:T(8,128)S(1)} all-to-all(f32[8,16,128]{2,1,0:T(8,128)S(1)} %get-tuple-element.16), channel_id=1, replica_groups=mesh['sky'=4,'exp'=8] {'exp'}, dimensions={0} | all-to-all | bytes 131072 | tf_op jit(solution)/shard_map/all_to_all | solution.py:280
  36.0 0.0 copy-done.4
  36.0 1.3 %shard_map.70 = f32[32,8,128]{2,1,0:T(8,128)S(1)} custom-call(f32[8,16,128]{2,1,0:T(8,128)S(1)} %all_to_all.31.values_ref.first_ref, s32[1,1,8,1024]{3,2,1,0:T(8,128)S(1)} %copy-done.4, f32[8,1024]{1,0:T(8,128)S(1)} %get-tuple-element.17.live_ref, f32[32,128]{1,0:T(8,128)S(1)} %get-tuple-element.18.scale_ref), custom_call_target="tpu_custom_call" | custom-call | flops 2000000000 | bytes 1048576 | tf_op jit(solution)/shard_map/pallas_call | solution.py:295
  37.3 10.2 %all_to_all.32.arrived_ref = f32[32,8,128]{2,1,0:T(8,128)S(1)} all-to-all(f32[32,8,128]{2,1,0:T(8,128)S(1)} %shard_map.70), channel_id=1, replica_groups=mesh['sky'=4,'exp'=8] {'sky','exp'}, dimensions={0} | all-to-all | bytes 262144 | tf_op jit(solution)/shard_map/all_to_all | solution.py:277
  47.4 5.2 %shard_map.71 = (f32[8,16,128]{2,1,0:T(8,128)S(1)}, f32[96,128]{1,0:T(8,128)S(1)}) custom-call(f32[32,8,128]{2,1,0:T(8,128)S(1)} %all_to_all.32.arrived_ref, s32[32,1024]{1,0:T(8,128)S(1)} %get-tuple-element.19.all_ref, f32[96,128]{1,0:T(8,128)S(1)} %get-tuple-element.20.right_ref, s32[1,1,8,1024]{3,2,1,0:T(8,128)S(1)} %copy-done), custom_call_target="tpu_custom_call" | custom-call | flops 2000000000 | bytes 1048576 | tf_op jit(solution)/shard_map/pallas_call | solution.py:297
  52.7 8.3 %all_to_all.33.second_ref = f32[8,16,128]{2,1,0:T(8,128)S(1)} all-to-all(f32[8,16,128]{2,1,0:T(8,128)S(1)} %get-tuple-element.21), channel_id=1, replica_groups=mesh['sky'=4,'exp'=8] {'exp'}, dimensions={0} | all-to-all | bytes 131072 | tf_op jit(solution)/shard_map/all_to_all | solution.py:280
  60.9 1.4 %shard_map.72 = (f32[32,1152]{1,0:T(8,128)S(1)}, f32[96,128]{1,0:T(8,128)S(1)}, f32[8,128]{1,0:T(8,128)S(1)}) custom-call(f32[8,16,128]{2,1,0:T(8,128)S(1)} %all_to_all.31.values_ref.first_ref, f32[8,16,128]{2,1,0:T(8,128)S(1)} %all_to_all.33.second_ref, s32[1,1,8,1024]{3,2,1,0:T(8,128)S(1)} %copy-done.4, f32[8,1024]{1,0:T(8,128)S(1)} %get-tuple-element.17.live_ref, ...), custom_call_target="tpu_custom_call" | custom-call | flops 2000000000 | bytes 1048576 | tf_op jit(solution)/shard_map/pallas_call | solution.py:299
  62.3 0.2 copy.7
  62.5 10.0 %all_to_all.34 = f32[32,1,1152]{2,1,0:T(1,128)S(1)} all-to-all(f32[32,1,1152]{2,1,0:T(1,128)S(1)} %copy.7), channel_id=1, replica_groups=mesh['sky'=4,'exp'=8] {'sky','exp'}, dimensions={0} | all-to-all | bytes 294912 | tf_op jit(solution)/shard_map/all_to_all | solution.py:277
  72.5 4.9 %shard_map.73 = (f32[96,128]{1,0:T(8,128)}, f32[96,128]{1,0:T(8,128)}) custom-call(f32[32,1152]{1,0:T(8,128)S(1)} %bitcast.9, s32[32,1024]{1,0:T(8,128)S(1)} %get-tuple-element.19.all_ref, f32[96,128]{1,0:T(8,128)S(1)} %get-tuple-element.20.right_ref, f32[96,128]{1,0:T(8,128)S(1)} %get-tuple-element.22.image_ref, ...), custom_call_target="tpu_custom_call" | custom-call | flops 2000000000 | bytes 1048576 | tf_op jit(solution)/shard_map/pallas_call | solution.py:303
  (1 shorter events, 0.0 us)
Async XLA Ops:
  0.6 0.8 copy-start.1
  1.4 0.8 copy-start.2
  2.1 0.8 copy-start.3
  2.9 0.7 copy-start.5
  5.9 7.3 %copy-start = (s32[1,1,8,1024]{3,2,1,0:T(8,128)S(1)}, s32[1,1,8,1024]{3,2,1,0:T(8,128)}, u32[]{:S(2)}) copy-start(s32[1,1,8,1024]{3,2,1,0:T(8,128)} %zp_ref.1) | copy-start | bytes 98308
  5.9 15.5 %all-to-all-start = ((f32[32,8,128]{2,1,0:T(8,128)}), f32[32,8,128]{2,1,0:T(8,128)S(1)}, u32[]{:S(2)}, u32[]{:S(2)}) async-start(f32[32,8,128]{2,1,0:T(8,128)} %get-tuple-element.15), calls=%async_computation | async-start | bytes 262144 | tf_op jit(solution)/shard_map/all_to_all | solution.py:277
  13.2 5.1 %collective-permute-start.2 = (s32[1,1,8,1024]{3,2,1,0:T(8,128)S(1)}, s32[1,1,8,1024]{3,2,1,0:T(8,128)S(1)}, u32[]{:S(2)}, u32[]{:S(2)}) collective-permute-start(s32[1,1,8,1024]{3,2,1,0:T(8,128)S(1)} %copy-done), channel_id=1, source_target_pairs={{0,24},{8,16},{16,8},{24,0},{1,25},{9,17},{17,9},{25,1},{2,26},{10... | collective-permute-start | bytes 98312 | tf_op jit(solution)/shard_map/ppermute | solution.py:282
  16.0 4.1 %collective-permute-start.1 = (s32[1,1,8,1024]{3,2,1,0:T(8,128)S(1)}, s32[1,1,8,1024]{3,2,1,0:T(8,128)S(1)}, u32[]{:S(2)}, u32[]{:S(2)}) collective-permute-start(s32[1,1,8,1024]{3,2,1,0:T(8,128)S(1)} %copy-done), channel_id=1, source_target_pairs={{0,16},{8,24},{16,0},{24,8},{1,17},{9,25},{17,1},{25,9},{2,18},{10... | collective-permute-start | bytes 98312 | tf_op jit(solution)/shard_map/ppermute | solution.py:282
  16.5 4.0 %collective-permute-start = (s32[1,1,8,1024]{3,2,1,0:T(8,128)S(1)}, s32[1,1,8,1024]{3,2,1,0:T(8,128)S(1)}, u32[]{:S(2)}, u32[]{:S(2)}) collective-permute-start(s32[1,1,8,1024]{3,2,1,0:T(8,128)S(1)} %copy-done), channel_id=1, source_target_pairs={{0,8},{8,0},{16,24},{24,16},{1,9},{9,1},{17,25},{25,17},{2,10},{10... | collective-permute-start | bytes 98312 | tf_op jit(solution)/shard_map/ppermute | solution.py:282
  26.6 9.4 %copy-start.4 = (s32[1,1,8,1024]{3,2,1,0:T(8,128)S(1)}, s32[1,1,8,1024]{3,2,1,0:T(8,128)}, u32[]{:S(2)}) copy-start(s32[1,1,8,1024]{3,2,1,0:T(8,128)} %star_ref.5) | copy-start | bytes 98308

commit v2 on v1

--- a/solution.py
+++ b/solution.py
@@ -19,21 +19,25 @@
 i16 = jnp.int16
 STAR_ROWS = STAR_DEV // LANES
 ZP_ROWS = -(-ZP_DEV // (LANES * 16)) * 16
-CONTRACT_LANES = (((1,), (1,)), ((), ()))
-
-
-def hot_rows(index, values, rows):
+WIDE_ROWS, WIDE_COLUMNS = 64, 192
+
+
+def hot_rows(upper_index, lower_index, values, rows, columns):
     position = lax.broadcasted_iota(i16, (16, LANES), 0)
-    high = jnp.broadcast_to(index >> 7, (16, LANES)).astype(i16)
-    low = jnp.broadcast_to(index & 127, (16, LANES)).astype(i16)
+    high = jnp.broadcast_to(upper_index, (16, LANES)).astype(i16)
     one, zero = jnp.ones((), bf16), jnp.zeros((), bf16)
     masks = [position + jnp.int16(16 * step) == high for step in range(rows // 16)]
     upper = []
     for value in values:
         spread = jnp.broadcast_to(value, (16, LANES)).astype(bf16)
         upper.extend(jnp.where(mask, spread, zero) for mask in masks)
-    lower = [jnp.where(position + jnp.int16(16 * step) == low, one, zero) for step in range(LANES // 16)]
-    return jnp.concatenate(upper, 0), jnp.concatenate(lower, 0)
+    low = jnp.broadcast_to(lower_index.astype(f32), (LANES, LANES)).astype(bf16).T
+    lane = lax.broadcasted_iota(jnp.int32, (LANES, LANES), 1).astype(f32).astype(bf16)
+    lower = [
+        jnp.where(low == lane + jnp.asarray(start, bf16), one, zero)[:, :min(LANES, columns - start)]
+        for start in range(0, columns, LANES)
+    ]
+    return jnp.concatenate(upper, 0), jnp.concatenate(lower, 1)
 
 
 def halves(value):
@@ -41,15 +45,15 @@
     return [top, value - top]
 
 
-def sum_rows(pairs, rows):
+def sum_rows(entries, rows, columns):
     uppers, lowers = [], []
-    for index, values in pairs:
+    for upper_index, lower_index, values in entries:
         parts = [part for value in values for part in halves(value)]
-        upper, lower = hot_rows(index, parts, rows)
+        upper, lower = hot_rows(upper_index, lower_index, parts, rows, columns)
         uppers.append(upper)
         lowers.append(lower)
-    total = lax.dot_general(jnp.concatenate(uppers, 1), jnp.concatenate(lowers, 1), CONTRACT_LANES, preferred_element_type=f32)
-    return [total[2 * n * rows:(2 * n + 1) * rows] + total[(2 * n + 1) * rows:(2 * n + 2) * rows] for n in range(len(pairs[0][1]))]
+    total = jnp.dot(jnp.concatenate(uppers, 1), jnp.concatenate(lowers, 0), preferred_element_type=f32)
+    return [total[2 * n * rows:(2 * n + 1) * rows] + total[(2 * n + 1) * rows:(2 * n + 2) * rows] for n in range(len(entries[0][2]))]
 
 
 def pick(table_ref, index, rows):
@@ -84,20 +88,31 @@
     def block(g, carry):
         stars = star_ref[pl.ds(pl.multiple_of(g * SUB, SUB), SUB), :]
         values = [ref[pl.ds(pl.multiple_of(g * SUB, SUB), SUB), :] for ref in value_refs]
+        high, low = stars >> 7, stars & 127
         pairs = []
         for r in range(SUB):
             for a in range(cap // LANES):
                 cut = (slice(r, r + 1), slice(a * LANES, (a + 1) * LANES))
-                pairs.append((stars[cut], [value[cut] for value in values]))
-        for ref, part in zip(sums_refs, sum_rows(pairs, STAR_ROWS)):
+                pairs.append((high[cut], low[cut], [value[cut] for value in values]))
+        for ref, part in zip(sums_refs, sum_rows(pairs, STAR_ROWS, LANES)):
             ref[...] += part
         return carry
 
     lax.fori_loop(0, n_rows // SUB, block, 0)
 
 
-def first_terms(n_sky, count_ref, weight_ref, magnitude_ref, star_ref, terms_ref, live_ref, scale_ref, moment_ref, sums_ref, mean_ref):
-    n_rows, cap = weight_ref.shape[2:]
+def first_terms(n_sky, count_ref, weight_from, magnitude_from, star_from, terms_ref, live_ref, scale_ref,
+                weight_ref, magnitude_ref, star_ref, moment_ref, sums_ref, mean_ref, arrival):
+    n_rows, cap = weight_from.shape[2:]
+    copies = [
+        pltpu.make_async_copy(source, target, arrival.at[n])
+        for n, (source, target) in enumerate(
+            [(weight_from, weight_ref), (magnitude_from, magnitude_ref), (star_from, star_ref)])
+    ]
+    for copy in copies:
+        copy.start()
+    for copy in copies:
+        copy.wait()
     sub = lax.broadcasted_iota(jnp.int32, (SUB, LANES), 0)
     lane = lax.broadcasted_iota(jnp.int32, (SUB, LANES), 1)
     for g in range(n_rows // SUB):
@@ -121,37 +136,41 @@
                 terms_ref[i * n_rows + g * SUB:i * n_rows + (g + 1) * SUB, a, :] = term
 
 
-def owner_sums(zp_ref, arrived, n_groups, cap, total_ref):
-    total_ref[...] = jnp.zeros_like(total_ref)
+def owner_sums(zp_ref, arrived, n_groups, cap, total_ref, wide_ref):
+    wide_ref[...] = jnp.zeros_like(wide_ref)
 
     def block(g, carry):
         index = zp_ref[pl.ds(pl.multiple_of(g * SUB, SUB), SUB), :]
+        row, lane = index >> 7, index & 127
+        beyond = row >= WIDE_ROWS
+        high = jnp.where(beyond, row - WIDE_ROWS + ((lane >> 6) << 5), row)
+        low = jnp.where(beyond, LANES + (lane & 63), lane)
         pairs = []
         for r in range(SUB):
             for a in range(cap // LANES):
-                pairs.append((index[r:r + 1, a * LANES:(a + 1) * LANES], [arrived(g, r, a)]))
-        total_ref[...] += sum_rows(pairs, ZP_ROWS)[0]
+                cut = (slice(r, r + 1), slice(a * LANES, (a + 1) * LANES))
+                pairs.append((high[cut], low[cut], [arrived(g, r, a)]))
+        wide_ref[...] += sum_rows(pairs, WIDE_ROWS, WIDE_COLUMNS)[0]
         return carry
 
     lax.fori_loop(0, n_groups, block, 0)
+    total_ref[0:WIDE_ROWS, :] = wide_ref[:, 0:LANES]
+    total_ref[WIDE_ROWS:ZP_ROWS, :] = jnp.concatenate(
+        [wide_ref[0:WIDE_ROWS // 2, LANES:WIDE_COLUMNS], wide_ref[WIDE_ROWS // 2:WIDE_ROWS, LANES:WIDE_COLUMNS]], 1)
 
 
 def send_picks(zp_ref, table_ref, out_ref, scalar):
     n_rows, cap = zp_ref.shape[2:]
     for g in range(n_rows // SUB):
-
-        def one(a, carry, g=g):
-            lanes = pl.ds(pl.multiple_of(a * LANES, LANES), LANES)
-            index = zp_ref[0, 0, g * SUB:(g + 1) * SUB, lanes]
-            out_ref[g * SUB:(g + 1) * SUB, pl.ds(a, 1), :] = pick(table_ref, index, ZP_ROWS).reshape(SUB, 1, LANES)
-            return carry
-
-        lax.fori_loop(0, cap // LANES, one, 0, unroll=2)
+        rows = slice(g * SUB, (g + 1) * SUB)
+        for a in range(cap // LANES):
+            index = zp_ref[0, 0, rows, a * LANES:(a + 1) * LANES]
+            out_ref[rows, a, :] = pick(table_ref, index, ZP_ROWS)
     out_ref[:, cap // LANES, :] = jnp.broadcast_to(scalar, (n_rows, LANES))
 
 
 def first_owner(n_sky, me_ref, arrived_ref, *refs):
-    zp_refs, (sent_ref, all_ref, right_ref) = refs[:n_sky], refs[n_sky:]
+    zp_refs, (sent_ref, all_ref, right_ref, wide_ref) = refs[:n_sky], refs[n_sky:]
     n_rows, cap = zp_refs[0].shape[2:]
     for d in range(n_sky):
         start = pl.multiple_of((me_ref[0] ^ d) * n_rows, SUB)
@@ -160,7 +179,7 @@
     def arrived(g, r, a):
         return arrived_ref[pl.ds(g * SUB + r, 1), a, :]
 
-    owner_sums(all_ref, arrived, n_sky * n_rows // SUB, cap, right_ref)
+    owner_sums(all_ref, arrived, n_sky * n_rows // SUB, cap, right_ref, wide_ref)
     right = right_ref[...]
     send_picks(zp_refs[0], right_ref, sent_ref, whole_sum(right * right))
 
@@ -194,13 +213,13 @@
     star_terms(n_sky, star_ref, live_ref, scale_ref, slot_ref, product_ref, sums_ref, mean_ref, emit)
 
 
-def second_owner(arrived_ref, all_ref, right_ref, zp_ref, sent_ref, image_ref):
+def second_owner(arrived_ref, all_ref, right_ref, zp_ref, sent_ref, image_ref, wide_ref):
     n_rows, cap = zp_ref.shape[2:]
 
     def arrived(g, r, a):
         return arrived_ref[pl.ds(g * SUB + r, 1), a, :]
 
-    owner_sums(all_ref, arrived, all_ref.shape[0] // SUB, cap, image_ref)
+    owner_sums(all_ref, arrived, all_ref.shape[0] // SUB, cap, image_ref, wide_ref)
     right = right_ref[...]
     image_ref[...] = image_ref[...] + ridge * right
     send_picks(zp_ref, image_ref, sent_ref, whole_sum(right * image_ref[...]))
@@ -232,13 +251,13 @@
     terms_ref[:, cap:cap + LANES] = jnp.broadcast_to(both, (n_sky * n_rows, LANES))
 
 
-def last_owner(arrived_ref, all_ref, right_ref, image_ref, residual_ref, scalar_ref, points_ref, left_ref, total_ref):
+def last_owner(arrived_ref, all_ref, right_ref, image_ref, residual_ref, scalar_ref, points_ref, left_ref, total_ref, wide_ref):
     cap = all_ref.shape[1]
 
     def arrived(g, r, a):
         return arrived_ref[pl.ds(pl.multiple_of(g * SUB, SUB), SUB), a * LANES:(a + 1) * LANES][r:r + 1]
 
-    owner_sums(all_ref, arrived, all_ref.shape[0] // SUB, cap, total_ref)
+    owner_sums(all_ref, arrived, all_ref.shape[0] // SUB, cap, total_ref, wide_ref)
     sums = jnp.sum(arrived_ref[:, cap:cap + LANES], axis=0, keepdims=True)
     norm_next = sums[:, LANES // 2:LANES // 2 + 1]
     product = sums[:, 0:1] + ridge * norm_next
@@ -269,6 +288,7 @@
     tall, star, slots = (ZP_ROWS, LANES), (STAR_ROWS, LANES), (n_exp, cap)
     terms = (n_sky * n_exp, cap // LANES, LANES)
     picks = (n_exp, 2 * SUB, LANES)
+    wide = (WIDE_ROWS, WIDE_COLUMNS)
     vmem = pl.BlockSpec(memory_space=pltpu.VMEM)
     smem = pl.BlockSpec(memory_space=pltpu.SMEM)
     me = jnp.reshape(lax.axis_index("sky"), (1,)).astype(jnp.int32)
@@ -280,27 +300,35 @@
         return lax.all_to_all(x, "exp", split_axis=0, concat_axis=0, tiled=True)
 
     zp = [zp_index] + [lax.ppermute(zp_index, "sky", [(i, i ^ d) for i in range(n_sky)]) for d in range(1, n_sky)]
-    sent, live, scale = call(
-        functools.partial(first_terms, n_sky), [terms, slots, star], [slots, star, star],
-        in_specs=[smem, vmem, vmem, vmem],
+    anywhere = pl.BlockSpec(memory_space=pl.ANY)
+    whole = (1, 1, n_exp, cap)
+    sent, live, scale = pl.pallas_call(
+        functools.partial(first_terms, n_sky),
+        out_shape=[jax.ShapeDtypeStruct(shape, f32) for shape in (terms, slots, star)],
+        in_specs=[smem, anywhere, anywhere, anywhere],
+        scratch_shapes=[pltpu.VMEM(whole, f32), pltpu.VMEM(whole, f32), pltpu.VMEM(whole, jnp.int32),
+                        pltpu.VMEM(slots, f32), pltpu.VMEM(star, f32), pltpu.VMEM(star, f32), pltpu.SemaphoreType.DMA((3,))],
+        compiler_params=pltpu.CompilerParams(vmem_limit_bytes=58 << 20),
+        cost_estimate=pl.CostEstimate(flops=2_000_000_000, bytes_accessed=1 << 20, transcendentals=0),
     )(peer_count, obs_weight, magnitude, star_id)
     arrived = to_owners(sent)
     sent, zp_all, right = pl.pallas_call(
         functools.partial(first_owner, n_sky),
         out_shape=[jax.ShapeDtypeStruct(picks, f32), jax.ShapeDtypeStruct((n_sky * n_exp, cap), jnp.int32), jax.ShapeDtypeStruct(tall, f32)],
         in_specs=[smem] + [vmem] * (n_sky + 1),
+        scratch_shapes=[pltpu.VMEM(wide, f32)],
         compiler_params=pltpu.CompilerParams(vmem_limit_bytes=40 << 20),
     )(me, arrived, *zp)
     first = to_sources(sent)
     (sent,) = call(functools.partial(second_terms, n_sky), [terms], [slots, slots, star, star])(first, star_id, live, scale)
     arrived = to_owners(sent)
-    sent, image = call(second_owner, [picks, tall])(arrived, zp_all, right, zp_index)
+    sent, image = call(second_owner, [picks, tall], [wide])(arrived, zp_all, right, zp_index)
     second = to_sources(sent)
     sent, residual, scalars = call(
         functools.partial(third_terms, n_sky), [(n_sky * n_exp, cap + LANES), tall, (SUB, LANES)], [slots, slots, star, star]
     )(first, second, star_id, live, scale, right, image)
     arrived = to_owners(sent)
-    points, left = call(last_owner, [tall, tall], [tall])(arrived, zp_all, right, image, residual, scalars)
+    points, left = call(last_owner, [tall, tall], [tall, wide])(arrived, zp_all, right, image, residual, scalars)
     return points.reshape(-1)[:ZP_DEV], left.reshape(-1)[:ZP_DEV]
 
 

time: 78 us -> 73 us (0.936)
  local copies, waits for them, and re-layouts: 3.09 us -> 0.19 us
  Pallas kernels: 20.3 us -> 18.2 us
    unnamed x13 -> x9, local copies, waits for them, and re-layouts: 2.94 us -> 0.04 us
    pallas_call x1, Pallas kernels: 5.21 us -> 4.17 us  [body(): pl.pallas_call(functools.partial(first_owner, n_sky), out_shape=[jax.Shap...]
    pallas_call x3, Pallas kernels: 12.5 us -> 11.6 us  [the longest x1 4.16 us: body(): call(second_owner, [picks, tall], [wide])(arrived, zp_all, right, zp_index)]
where the time goes in v2:
time: 73 us; the launch traced here: 72.5 us
  blocking collectives  38 us (52%)
  Pallas kernels  18.2 us (25%)
  starting transfers between devices  10.9 us (15%)
  waiting for transfers between devices  4.61 us (6%)
    all_to_all x2, blocking collectives, to_owners(): lax.all_to_all(x, ('sky', 'exp'), split_axis=0, concat_axis=0, tiled=True)  20.2 us
    all_to_all x2, blocking collectives, to_sources(): return lax.all_to_all(x, 'exp', split_axis=0, concat_axis=0, tiled=True)  17.8 us
    all_to_all x1, starting transfers between devices, to_owners(): lax.all_to_all(x, ('sky', 'exp'), split_axis=0, concat_axis=0, tiled=True)  7.3 us
    pallas_call x1, Pallas kernels, body(): pl.pallas_call(functools.partial(first_owner, n_sky), out_shape=[jax.Shap...  4.17 us
    pallas_call x1, Pallas kernels, body(): call(second_owner, [picks, tall], [wide])(arrived, zp_all, right, zp_index)  4.16 us
    pallas_call x1, Pallas kernels, body(): call(last_owner, [tall, tall], [tall, wide])  4.13 us
    ppermute x3, waiting for transfers between devices, body(): lax.ppermute(zp_index, 'sky', [(i, i ^ d) for i in range(n_sky)])  3.73 us
    ppermute x3, starting transfers between devices, body(): lax.ppermute(zp_index, 'sky', [(i, i ^ d) for i in range(n_sky)])  3.55 us
  transfers between devices with their start and end apart: 4, of which 4 were waited for; matrix products, arithmetic and copies ran while one was open for 0% of the time, Pallas kernels for 0%

profile of v2, /device:TPU:0, one launch (start us, length us, event | category | flops | bytes accessed | tf_op | source)
XLA Modules:
  0.0 72.5 jit_solution(7535039307245383357)
XLA Ops:
  0.6 3.3 %shard_map.68 = (f32[32,8,128]{2,1,0:T(8,128)}, f32[8,1024]{1,0:T(8,128)}, f32[32,128]{1,0:T(8,128)}) custom-call(s32[1,1,8]{2,1,0:T(1,128)} %count_ref.1, f32[1,1,8,1024]{3,2,1,0:T(8,128)} %weight_from.1, f32[1,1,8,1024]{3,2,1,0:T(8,128)} %magnitude_from.1, s32[1,1,8,1024]{3,2,1,0:T(8,128)} %star_ref.3), custom_call_target="tpu_custom_call" | custom-call | flops 2000000000 | bytes 1048576 | tf_op jit(solution)/shard_map/pallas_call | solution.py:305
  4.0 0.0 copy-start
  4.0 7.3 %all-to-all-start = ((f32[32,8,128]{2,1,0:T(8,128)}), f32[32,8,128]{2,1,0:T(8,128)S(1)}, u32[]{:S(2)}, u32[]{:S(2)}) async-start(f32[32,8,128]{2,1,0:T(8,128)} %get-tuple-element.15), calls=%async_computation | async-start | bytes 262144 | tf_op jit(solution)/shard_map/all_to_all | solution.py:297
  11.3 0.0 copy-done
  11.3 2.7 %collective-permute-start.2 = (s32[1,1,8,1024]{3,2,1,0:T(8,128)S(1)}, s32[1,1,8,1024]{3,2,1,0:T(8,128)S(1)}, u32[]{:S(2)}, u32[]{:S(2)}) collective-permute-start(s32[1,1,8,1024]{3,2,1,0:T(8,128)S(1)} %copy-done), channel_id=1, source_target_pairs={{0,24},{8,16},{16,8},{24,0},{1,25},{9,17},{17,9},{25,1},{2,26},{10... | collective-permute-start | bytes 98312 | tf_op jit(solution)/shard_map/ppermute | solution.py:302
  14.0 0.6 collective-permute-start.1
  14.6 0.3 collective-permute-start
  14.9 1.5 %collective-permute-done.2.refs_3_ = s32[1,1,8,1024]{3,2,1,0:T(8,128)S(1)} collective-permute-done((s32[1,1,8,1024]{3,2,1,0:T(8,128)S(1)}, s32[1,1,8,1024]{3,2,1,0:T(8,128)S(1)}, u32[]{:S(2)}, u32[]{:S(2)}) %collective-permute-start.2) | collective-permute-done | bytes 32800 | tf_op jit(solution)/shard_map/ppermute | solution.py:302
  16.4 1.8 %collective-permute-done.1.refs_2_ = s32[1,1,8,1024]{3,2,1,0:T(8,128)S(1)} collective-permute-done((s32[1,1,8,1024]{3,2,1,0:T(8,128)S(1)}, s32[1,1,8,1024]{3,2,1,0:T(8,128)S(1)}, u32[]{:S(2)}, u32[]{:S(2)}) %collective-permute-start.1) | collective-permute-done | bytes 32800 | tf_op jit(solution)/shard_map/ppermute | solution.py:302
  18.2 0.4 collective-permute-done.refs_1_
  18.6 0.9 %all-to-all-done.arrived_ref = f32[32,8,128]{2,1,0:T(8,128)S(1)} async-done(((f32[32,8,128]{2,1,0:T(8,128)}), f32[32,8,128]{2,1,0:T(8,128)S(1)}, u32[]{:S(2)}, u32[]{:S(2)}) %all-to-all-start) | async-done | bytes 131104 | tf_op jit(solution)/shard_map/all_to_all | solution.py:297
  19.5 4.2 %shard_map.69 = (f32[8,16,128]{2,1,0:T(8,128)S(1)}, s32[32,1024]{1,0:T(8,128)S(1)}, f32[96,128]{1,0:T(8,128)S(1)}) custom-call(s32[1]{0:T(128)} %bitcast.me_ref, f32[32,8,128]{2,1,0:T(8,128)S(1)} %all-to-all-done.arrived_ref, s32[1,1,8,1024]{3,2,1,0:T(8,128)S(1)} %copy-done, s32[1,1,8,1024]{3,2,1,0:T(8,128)S(1)} %collective-permute-done.refs_1_, ...), custom_call_target="tpu_custom_call" | custom-call | tf_op jit(solution)/shard_map/pallas_call | solution.py:315
  23.6 0.0 copy-start.1
  23.7 0.0 copy-start.2
  23.7 0.0 copy-start.3
  23.7 9.5 %all_to_all.31.values_ref.first_ref = f32[8,16,128]{2,1,0:T(8,128)S(1)} all-to-all(f32[8,16,128]{2,1,0:T(8,128)S(1)} %get-tuple-element.16), channel_id=1, replica_groups=mesh['sky'=4,'exp'=8] {'exp'}, dimensions={0} | all-to-all | bytes 131072 | tf_op jit(solution)/shard_map/all_to_all | solution.py:300
  33.2 0.0 copy-done.1
  33.2 0.0 copy-done.2
  33.2 0.0 copy-done.3
  33.2 1.1 %shard_map.70 = f32[32,8,128]{2,1,0:T(8,128)S(1)} custom-call(f32[8,16,128]{2,1,0:T(8,128)S(1)} %all_to_all.31.values_ref.first_ref, s32[1,1,8,1024]{3,2,1,0:T(8,128)S(1)} %copy-done.1, f32[8,1024]{1,0:T(8,128)S(1)} %copy-done.2, f32[32,128]{1,0:T(8,128)S(1)} %copy-done.3), custom_call_target="tpu_custom_call" | custom-call | flops 2000000000 | bytes 1048576 | tf_op jit(solution)/shard_map/pallas_call | solution.py:323
  34.3 10.2 %all_to_all.32.arrived_ref = f32[32,8,128]{2,1,0:T(8,128)S(1)} all-to-all(f32[32,8,128]{2,1,0:T(8,128)S(1)} %shard_map.70), channel_id=1, replica_groups=mesh['sky'=4,'exp'=8] {'sky','exp'}, dimensions={0} | all-to-all | bytes 262144 | tf_op jit(solution)/shard_map/all_to_all | solution.py:297
  44.5 4.2 %shard_map.71 = (f32[8,16,128]{2,1,0:T(8,128)S(1)}, f32[96,128]{1,0:T(8,128)S(1)}) custom-call(f32[32,8,128]{2,1,0:T(8,128)S(1)} %all_to_all.32.arrived_ref, s32[32,1024]{1,0:T(8,128)S(1)} %get-tuple-element.19.all_ref, f32[96,128]{1,0:T(8,128)S(1)} %get-tuple-element.20.right_ref, s32[1,1,8,1024]{3,2,1,0:T(8,128)S(1)} %copy-done), custom_call_target="tpu_custom_call" | custom-call | flops 2000000000 | bytes 1048576 | tf_op jit(solution)/shard_map/pallas_call | solution.py:325
  48.6 8.3 %all_to_all.33.second_ref = f32[8,16,128]{2,1,0:T(8,128)S(1)} all-to-all(f32[8,16,128]{2,1,0:T(8,128)S(1)} %get-tuple-element.21), channel_id=1, replica_groups=mesh['sky'=4,'exp'=8] {'exp'}, dimensions={0} | all-to-all | bytes 131072 | tf_op jit(solution)/shard_map/all_to_all | solution.py:300
  56.9 1.3 %shard_map.72 = (f32[32,1152]{1,0:T(8,128)S(1)}, f32[96,128]{1,0:T(8,128)S(1)}, f32[8,128]{1,0:T(8,128)S(1)}) custom-call(f32[8,16,128]{2,1,0:T(8,128)S(1)} %all_to_all.31.values_ref.first_ref, f32[8,16,128]{2,1,0:T(8,128)S(1)} %all_to_all.33.second_ref, s32[1,1,8,1024]{3,2,1,0:T(8,128)S(1)} %copy-done.1, f32[8,1024]{1,0:T(8,128)S(1)} %copy-done.2, ...), custom_call_target="tpu_custom_call" | custom-call | flops 2000000000 | bytes 1048576 | tf_op jit(solution)/shard_map/pallas_call | solution.py:327
  58.2 0.2 copy.7
  58.4 10.0 %all_to_all.34 = f32[32,1,1152]{2,1,0:T(1,128)S(1)} all-to-all(f32[32,1,1152]{2,1,0:T(1,128)S(1)} %copy.7), channel_id=1, replica_groups=mesh['sky'=4,'exp'=8] {'sky','exp'}, dimensions={0} | all-to-all | bytes 294912 | tf_op jit(solution)/shard_map/all_to_all | solution.py:297
  68.4 4.1 %shard_map.73 = (f32[96,128]{1,0:T(8,128)}, f32[96,128]{1,0:T(8,128)}) custom-call(f32[32,1152]{1,0:T(8,128)S(1)} %bitcast.9, s32[32,1024]{1,0:T(8,128)S(1)} %get-tuple-element.19.all_ref, f32[96,128]{1,0:T(8,128)S(1)} %get-tuple-element.20.right_ref, f32[96,128]{1,0:T(8,128)S(1)} %get-tuple-element.22.image_ref, ...), custom_call_target="tpu_custom_call" | custom-call | flops 2000000000 | bytes 1048576 | tf_op jit(solution)/shard_map/pallas_call | solution.py:331
  (1 shorter events, 0.0 us)
Async XLA Ops:
  4.0 7.3 %copy-start = (s32[1,1,8,1024]{3,2,1,0:T(8,128)S(1)}, s32[1,1,8,1024]{3,2,1,0:T(8,128)}, u32[]{:S(2)}) copy-start(s32[1,1,8,1024]{3,2,1,0:T(8,128)} %zp_ref.1) | copy-start | bytes 98308
  4.0 15.5 %all-to-all-start = ((f32[32,8,128]{2,1,0:T(8,128)}), f32[32,8,128]{2,1,0:T(8,128)S(1)}, u32[]{:S(2)}, u32[]{:S(2)}) async-start(f32[32,8,128]{2,1,0:T(8,128)} %get-tuple-element.15), calls=%async_computation | async-start | bytes 262144 | tf_op jit(solution)/shard_map/all_to_all | solution.py:297
  11.3 5.1 %collective-permute-start.2 = (s32[1,1,8,1024]{3,2,1,0:T(8,128)S(1)}, s32[1,1,8,1024]{3,2,1,0:T(8,128)S(1)}, u32[]{:S(2)}, u32[]{:S(2)}) collective-permute-start(s32[1,1,8,1024]{3,2,1,0:T(8,128)S(1)} %copy-done), channel_id=1, source_target_pairs={{0,24},{8,16},{16,8},{24,0},{1,25},{9,17},{17,9},{25,1},{2,26},{10... | collective-permute-start | bytes 98312 | tf_op jit(solution)/shard_map/ppermute | solution.py:302
  14.0 4.1 %collective-permute-start.1 = (s32[1,1,8,1024]{3,2,1,0:T(8,128)S(1)}, s32[1,1,8,1024]{3,2,1,0:T(8,128)S(1)}, u32[]{:S(2)}, u32[]{:S(2)}) collective-permute-start(s32[1,1,8,1024]{3,2,1,0:T(8,128)S(1)} %copy-done), channel_id=1, source_target_pairs={{0,16},{8,24},{16,0},{24,8},{1,17},{9,25},{17,1},{25,9},{2,18},{10... | collective-permute-start | bytes 98312 | tf_op jit(solution)/shard_map/ppermute | solution.py:302
  14.6 4.0 %collective-permute-start = (s32[1,1,8,1024]{3,2,1,0:T(8,128)S(1)}, s32[1,1,8,1024]{3,2,1,0:T(8,128)S(1)}, u32[]{:S(2)}, u32[]{:S(2)}) collective-permute-start(s32[1,1,8,1024]{3,2,1,0:T(8,128)S(1)} %copy-done), channel_id=1, source_target_pairs={{0,8},{8,0},{16,24},{24,16},{1,9},{9,1},{17,25},{25,17},{2,10},{10... | collective-permute-start | bytes 98312 | tf_op jit(solution)/shard_map/ppermute | solution.py:302
  23.6 9.5 %copy-start.1 = (s32[1,1,8,1024]{3,2,1,0:T(8,128)S(1)}, s32[1,1,8,1024]{3,2,1,0:T(8,128)}, u32[]{:S(2)}) copy-start(s32[1,1,8,1024]{3,2,1,0:T(8,128)} %star_ref.3) | copy-start | bytes 98308
  23.7 9.5 %copy-start.2 = (f32[8,1024]{1,0:T(8,128)S(1)}, f32[8,1024]{1,0:T(8,128)}, u32[]{:S(2)}) copy-start(f32[8,1024]{1,0:T(8,128)} %get-tuple-element.17.live_ref) | copy-start | bytes 98308
  23.7 9.5 %copy-start.3 = (f32[32,128]{1,0:T(8,128)S(1)}, f32[32,128]{1,0:T(8,128)}, u32[]{:S(2)}) copy-start(f32[32,128]{1,0:T(8,128)} %get-tuple-element.18.scale_ref) | copy-start | bytes 49156

commit v3 on v2

--- a/solution.py
+++ b/solution.py
@@ -1,4 +1,5 @@
 import functools
+import math
 
 import jax
 import jax.numpy as jnp
@@ -19,7 +20,8 @@
 i16 = jnp.int16
 STAR_ROWS = STAR_DEV // LANES
 ZP_ROWS = -(-ZP_DEV // (LANES * 16)) * 16
-WIDE_ROWS, WIDE_COLUMNS = 64, 192
+HALF_ROWS = ZP_ROWS // 2
+OWNER_BLOCK = 32
 
 
 def hot_rows(upper_index, lower_index, values, rows, columns):
@@ -136,50 +138,57 @@
                 terms_ref[i * n_rows + g * SUB:i * n_rows + (g + 1) * SUB, a, :] = term
 
 
-def owner_sums(zp_ref, arrived, n_groups, cap, total_ref, wide_ref):
-    wide_ref[...] = jnp.zeros_like(wide_ref)
-
-    def block(g, carry):
-        index = zp_ref[pl.ds(pl.multiple_of(g * SUB, SUB), SUB), :]
-        row, lane = index >> 7, index & 127
-        beyond = row >= WIDE_ROWS
-        high = jnp.where(beyond, row - WIDE_ROWS + ((lane >> 6) << 5), row)
-        low = jnp.where(beyond, LANES + (lane & 63), lane)
-        pairs = []
-        for r in range(SUB):
-            for a in range(cap // LANES):
-                cut = (slice(r, r + 1), slice(a * LANES, (a + 1) * LANES))
-                pairs.append((high[cut], low[cut], [arrived(g, r, a)]))
-        wide_ref[...] += sum_rows(pairs, WIDE_ROWS, WIDE_COLUMNS)[0]
+def owner_sums(zp_ref, arrived, n_rows, cap, total_ref, most=OWNER_BLOCK):
+    total_ref[...] = jnp.zeros_like(total_ref)
+    step = math.gcd(n_rows, most)
+
+    def block(n, carry):
+        entries = []
+        for g in range(step // SUB):
+            first = pl.multiple_of(n * step + g * SUB, SUB)
+            index = zp_ref[pl.ds(first, SUB), :]
+            row, lane = index >> 7, index & 127
+            beyond = row >= HALF_ROWS
+            high = jnp.where(beyond, row - HALF_ROWS, row)
+            low = jnp.where(beyond, lane + LANES, lane)
+            for r in range(SUB):
+                for a in range(cap // LANES):
+                    cut = (slice(r, r + 1), slice(a * LANES, (a + 1) * LANES))
+                    entries.append((high[cut], low[cut], [arrived(first, r, a)]))
+        total = sum_rows(entries, HALF_ROWS, 2 * LANES)[0]
+        total_ref[0:HALF_ROWS, :] += total[:, 0:LANES]
+        total_ref[HALF_ROWS:ZP_ROWS, :] += total[:, LANES:2 * LANES]
         return carry
 
-    lax.fori_loop(0, n_groups, block, 0)
-    total_ref[0:WIDE_ROWS, :] = wide_ref[:, 0:LANES]
-    total_ref[WIDE_ROWS:ZP_ROWS, :] = jnp.concatenate(
-        [wide_ref[0:WIDE_ROWS // 2, LANES:WIDE_COLUMNS], wide_ref[WIDE_ROWS // 2:WIDE_ROWS, LANES:WIDE_COLUMNS]], 1)
+    lax.fori_loop(0, n_rows // step, block, 0)
 
 
 def send_picks(zp_ref, table_ref, out_ref, scalar):
     n_rows, cap = zp_ref.shape[2:]
     for g in range(n_rows // SUB):
         rows = slice(g * SUB, (g + 1) * SUB)
-        for a in range(cap // LANES):
-            index = zp_ref[0, 0, rows, a * LANES:(a + 1) * LANES]
-            out_ref[rows, a, :] = pick(table_ref, index, ZP_ROWS)
+
+        def one(a, carry, rows=rows):
+            lanes = pl.ds(pl.multiple_of(a * LANES, LANES), LANES)
+            index = zp_ref[0, 0, rows, lanes]
+            out_ref[rows, pl.ds(a, 1), :] = pick(table_ref, index, ZP_ROWS).reshape(SUB, 1, LANES)
+            return carry
+
+        lax.fori_loop(0, cap // LANES, one, 0, unroll=4)
     out_ref[:, cap // LANES, :] = jnp.broadcast_to(scalar, (n_rows, LANES))
 
 
 def first_owner(n_sky, me_ref, arrived_ref, *refs):
-    zp_refs, (sent_ref, all_ref, right_ref, wide_ref) = refs[:n_sky], refs[n_sky:]
+    zp_refs, (sent_ref, all_ref, right_ref) = refs[:n_sky], refs[n_sky:]
     n_rows, cap = zp_refs[0].shape[2:]
     for d in range(n_sky):
         start = pl.multiple_of((me_ref[0] ^ d) * n_rows, SUB)
         all_ref[pl.ds(start, n_rows), :] = zp_refs[d][0, 0]
 
-    def arrived(g, r, a):
-        return arrived_ref[pl.ds(g * SUB + r, 1), a, :]
-
-    owner_sums(all_ref, arrived, n_sky * n_rows // SUB, cap, right_ref, wide_ref)
+    def arrived(first, r, a):
+        return arrived_ref[pl.ds(first + r, 1), a, :]
+
+    owner_sums(all_ref, arrived, n_sky * n_rows, cap, right_ref, 32)
     right = right_ref[...]
     send_picks(zp_refs[0], right_ref, sent_ref, whole_sum(right * right))
 
@@ -213,13 +222,13 @@
     star_terms(n_sky, star_ref, live_ref, scale_ref, slot_ref, product_ref, sums_ref, mean_ref, emit)
 
 
-def second_owner(arrived_ref, all_ref, right_ref, zp_ref, sent_ref, image_ref, wide_ref):
+def second_owner(arrived_ref, all_ref, right_ref, zp_ref, sent_ref, image_ref):
     n_rows, cap = zp_ref.shape[2:]
 
-    def arrived(g, r, a):
-        return arrived_ref[pl.ds(g * SUB + r, 1), a, :]
-
-    owner_sums(all_ref, arrived, all_ref.shape[0] // SUB, cap, image_ref, wide_ref)
+    def arrived(first, r, a):
+        return arrived_ref[pl.ds(first + r, 1), a, :]
+
+    owner_sums(all_ref, arrived, all_ref.shape[0], cap, image_ref, 32)
     right = right_ref[...]
     image_ref[...] = image_ref[...] + ridge * right
     send_picks(zp_ref, image_ref, sent_ref, whole_sum(right * image_ref[...]))
@@ -251,13 +260,13 @@
     terms_ref[:, cap:cap + LANES] = jnp.broadcast_to(both, (n_sky * n_rows, LANES))
 
 
-def last_owner(arrived_ref, all_ref, right_ref, image_ref, residual_ref, scalar_ref, points_ref, left_ref, total_ref, wide_ref):
+def last_owner(arrived_ref, all_ref, right_ref, image_ref, residual_ref, scalar_ref, points_ref, left_ref, total_ref):
     cap = all_ref.shape[1]
 
-    def arrived(g, r, a):
-        return arrived_ref[pl.ds(pl.multiple_of(g * SUB, SUB), SUB), a * LANES:(a + 1) * LANES][r:r + 1]
-
-    owner_sums(all_ref, arrived, all_ref.shape[0] // SUB, cap, total_ref, wide_ref)
+    def arrived(first, r, a):
+        return arrived_ref[pl.ds(first, SUB), a * LANES:(a + 1) * LANES][r:r + 1]
+
+    owner_sums(all_ref, arrived, all_ref.shape[0], cap, total_ref)
     sums = jnp.sum(arrived_ref[:, cap:cap + LANES], axis=0, keepdims=True)
     norm_next = sums[:, LANES // 2:LANES // 2 + 1]
     product = sums[:, 0:1] + ridge * norm_next
@@ -288,7 +297,6 @@
     tall, star, slots = (ZP_ROWS, LANES), (STAR_ROWS, LANES), (n_exp, cap)
     terms = (n_sky * n_exp, cap // LANES, LANES)
     picks = (n_exp, 2 * SUB, LANES)
-    wide = (WIDE_ROWS, WIDE_COLUMNS)
     vmem = pl.BlockSpec(memory_space=pltpu.VMEM)
     smem = pl.BlockSpec(memory_space=pltpu.SMEM)
     me = jnp.reshape(lax.axis_index("sky"), (1,)).astype(jnp.int32)
@@ -316,19 +324,18 @@
         functools.partial(first_owner, n_sky),
         out_shape=[jax.ShapeDtypeStruct(picks, f32), jax.ShapeDtypeStruct((n_sky * n_exp, cap), jnp.int32), jax.ShapeDtypeStruct(tall, f32)],
         in_specs=[smem] + [vmem] * (n_sky + 1),
-        scratch_shapes=[pltpu.VMEM(wide, f32)],
         compiler_params=pltpu.CompilerParams(vmem_limit_bytes=40 << 20),
     )(me, arrived, *zp)
     first = to_sources(sent)
     (sent,) = call(functools.partial(second_terms, n_sky), [terms], [slots, slots, star, star])(first, star_id, live, scale)
     arrived = to_owners(sent)
-    sent, image = call(second_owner, [picks, tall], [wide])(arrived, zp_all, right, zp_index)
+    sent, image = call(second_owner, [picks, tall])(arrived, zp_all, right, zp_index)
     second = to_sources(sent)
     sent, residual, scalars = call(
         functools.partial(third_terms, n_sky), [(n_sky * n_exp, cap + LANES), tall, (SUB, LANES)], [slots, slots, star, star]
     )(first, second, star_id, live, scale, right, image)
     arrived = to_owners(sent)
-    points, left = call(last_owner, [tall, tall], [tall, wide])(arrived, zp_all, right, image, residual, scalars)
+    points, left = call(last_owner, [tall, tall], [tall])(arrived, zp_all, right, image, residual, scalars)
     return points.reshape(-1)[:ZP_DEV], left.reshape(-1)[:ZP_DEV]
 
 

time: 73 us -> 71.3 us (0.977)
  Pallas kernels: 18.2 us -> 16.5 us
    pallas_call x2, Pallas kernels: 8.29 us -> 7.16 us  [the longest x1 3.65 us: body(): call(second_owner, [picks, tall])(arrived, zp_all, right, zp_index)]
where the time goes in v3:
time: 71.3 us; the launch traced here: 70.9 us
  blocking collectives  38 us (53%)
  Pallas kernels  16.5 us (23%)
  starting transfers between devices  10.9 us (15%)
  waiting for transfers between devices  4.61 us (6%)
  between operations  0.73 us (1%)
    all_to_all x2, blocking collectives, to_owners(): lax.all_to_all(x, ('sky', 'exp'), split_axis=0, concat_axis=0, tiled=True)  20.2 us
    all_to_all x2, blocking collectives, to_sources(): return lax.all_to_all(x, 'exp', split_axis=0, concat_axis=0, tiled=True)  17.8 us
    all_to_all x1, starting transfers between devices, to_owners(): lax.all_to_all(x, ('sky', 'exp'), split_axis=0, concat_axis=0, tiled=True)  7.3 us
    ppermute x3, waiting for transfers between devices, body(): lax.ppermute(zp_index, 'sky', [(i, i ^ d) for i in range(n_sky)])  3.73 us
    pallas_call x1, Pallas kernels, body(): call(second_owner, [picks, tall])(arrived, zp_all, right, zp_index)  3.65 us
    pallas_call x1, Pallas kernels, body(): pl.pallas_call(functools.partial(first_owner, n_sky), out_shape=[jax.Shap...  3.63 us
    ppermute x3, starting transfers between devices, body(): lax.ppermute(zp_index, 'sky', [(i, i ^ d) for i in range(n_sky)])  3.55 us
    pallas_call x1, Pallas kernels, body(): call(last_owner, [tall, tall], [tall])  3.51 us
  transfers between devices with their start and end apart: 4, of which 4 were waited for; matrix products, arithmetic and copies ran while one was open for 0% of the time, Pallas kernels for 0%

profile of v3, /device:TPU:0, one launch (start us, length us, event | category | flops | bytes accessed | tf_op | source)
XLA Modules:
  0.0 70.9 jit_solution(10873030228537965150)
XLA Ops:
  0.6 3.3 %shard_map.68 = (f32[32,8,128]{2,1,0:T(8,128)}, f32[8,1024]{1,0:T(8,128)}, f32[32,128]{1,0:T(8,128)}) custom-call(s32[1,1,8]{2,1,0:T(1,128)} %count_ref.1, f32[1,1,8,1024]{3,2,1,0:T(8,128)} %weight_from.1, f32[1,1,8,1024]{3,2,1,0:T(8,128)} %magnitude_from.1, s32[1,1,8,1024]{3,2,1,0:T(8,128)} %star_ref.3), custom_call_target="tpu_custom_call" | custom-call | flops 2000000000 | bytes 1048576 | tf_op jit(solution)/shard_map/pallas_call | solution.py:313
  4.0 0.0 copy-start
  4.0 7.3 %all-to-all-start = ((f32[32,8,128]{2,1,0:T(8,128)}), f32[32,8,128]{2,1,0:T(8,128)S(1)}, u32[]{:S(2)}, u32[]{:S(2)}) async-start(f32[32,8,128]{2,1,0:T(8,128)} %get-tuple-element.15), calls=%async_computation | async-start | bytes 262144 | tf_op jit(solution)/shard_map/all_to_all | solution.py:305
  11.3 0.0 copy-done
  11.3 2.7 %collective-permute-start.2 = (s32[1,1,8,1024]{3,2,1,0:T(8,128)S(1)}, s32[1,1,8,1024]{3,2,1,0:T(8,128)S(1)}, u32[]{:S(2)}, u32[]{:S(2)}) collective-permute-start(s32[1,1,8,1024]{3,2,1,0:T(8,128)S(1)} %copy-done), channel_id=1, source_target_pairs={{0,24},{8,16},{16,8},{24,0},{1,25},{9,17},{17,9},{25,1},{2,26},{10... | collective-permute-start | bytes 98312 | tf_op jit(solution)/shard_map/ppermute | solution.py:310
  14.0 0.6 collective-permute-start.1
  14.6 0.3 collective-permute-start
  14.9 1.5 %collective-permute-done.2.refs_3_ = s32[1,1,8,1024]{3,2,1,0:T(8,128)S(1)} collective-permute-done((s32[1,1,8,1024]{3,2,1,0:T(8,128)S(1)}, s32[1,1,8,1024]{3,2,1,0:T(8,128)S(1)}, u32[]{:S(2)}, u32[]{:S(2)}) %collective-permute-start.2) | collective-permute-done | bytes 32800 | tf_op jit(solution)/shard_map/ppermute | solution.py:310
  16.4 1.8 %collective-permute-done.1.refs_2_ = s32[1,1,8,1024]{3,2,1,0:T(8,128)S(1)} collective-permute-done((s32[1,1,8,1024]{3,2,1,0:T(8,128)S(1)}, s32[1,1,8,1024]{3,2,1,0:T(8,128)S(1)}, u32[]{:S(2)}, u32[]{:S(2)}) %collective-permute-start.1) | collective-permute-done | bytes 32800 | tf_op jit(solution)/shard_map/ppermute | solution.py:310
  18.2 0.4 collective-permute-done.refs_1_
  18.6 0.9 %all-to-all-done.arrived_ref = f32[32,8,128]{2,1,0:T(8,128)S(1)} async-done(((f32[32,8,128]{2,1,0:T(8,128)}), f32[32,8,128]{2,1,0:T(8,128)S(1)}, u32[]{:S(2)}, u32[]{:S(2)}) %all-to-all-start) | async-done | bytes 131104 | tf_op jit(solution)/shard_map/all_to_all | solution.py:305
  19.5 3.6 %shard_map.69 = (f32[8,16,128]{2,1,0:T(8,128)S(1)}, s32[32,1024]{1,0:T(8,128)S(1)}, f32[96,128]{1,0:T(8,128)S(1)}) custom-call(s32[1]{0:T(128)} %bitcast.me_ref, f32[32,8,128]{2,1,0:T(8,128)S(1)} %all-to-all-done.arrived_ref, s32[1,1,8,1024]{3,2,1,0:T(8,128)S(1)} %copy-done, s32[1,1,8,1024]{3,2,1,0:T(8,128)S(1)} %collective-permute-done.refs_1_, ...), custom_call_target="tpu_custom_call" | custom-call | tf_op jit(solution)/shard_map/pallas_call | solution.py:323
  23.1 0.0 copy-start.1
  23.1 0.0 copy-start.2
  23.1 0.0 copy-start.3
  23.1 9.5 %all_to_all.31.values_ref.first_ref = f32[8,16,128]{2,1,0:T(8,128)S(1)} all-to-all(f32[8,16,128]{2,1,0:T(8,128)S(1)} %get-tuple-element.16), channel_id=1, replica_groups=mesh['sky'=4,'exp'=8] {'exp'}, dimensions={0} | all-to-all | bytes 131072 | tf_op jit(solution)/shard_map/all_to_all | solution.py:308
  32.6 0.0 copy-done.1
  32.6 0.0 copy-done.2
  32.7 0.0 copy-done.3
  32.7 1.1 %shard_map.70 = f32[32,8,128]{2,1,0:T(8,128)S(1)} custom-call(f32[8,16,128]{2,1,0:T(8,128)S(1)} %all_to_all.31.values_ref.first_ref, s32[1,1,8,1024]{3,2,1,0:T(8,128)S(1)} %copy-done.1, f32[8,1024]{1,0:T(8,128)S(1)} %copy-done.2, f32[32,128]{1,0:T(8,128)S(1)} %copy-done.3), custom_call_target="tpu_custom_call" | custom-call | flops 2000000000 | bytes 1048576 | tf_op jit(solution)/shard_map/pallas_call | solution.py:330
  33.8 10.2 %all_to_all.32.arrived_ref = f32[32,8,128]{2,1,0:T(8,128)S(1)} all-to-all(f32[32,8,128]{2,1,0:T(8,128)S(1)} %shard_map.70), channel_id=1, replica_groups=mesh['sky'=4,'exp'=8] {'sky','exp'}, dimensions={0} | all-to-all | bytes 262144 | tf_op jit(solution)/shard_map/all_to_all | solution.py:305
  43.9 3.6 %shard_map.71 = (f32[8,16,128]{2,1,0:T(8,128)S(1)}, f32[96,128]{1,0:T(8,128)S(1)}) custom-call(f32[32,8,128]{2,1,0:T(8,128)S(1)} %all_to_all.32.arrived_ref, s32[32,1024]{1,0:T(8,128)S(1)} %get-tuple-element.19.all_ref, f32[96,128]{1,0:T(8,128)S(1)} %get-tuple-element.20.right_ref, s32[1,1,8,1024]{3,2,1,0:T(8,128)S(1)} %copy-done), custom_call_target="tpu_custom_call" | custom-call | flops 2000000000 | bytes 1048576 | tf_op jit(solution)/shard_map/pallas_call | solution.py:332
  47.6 8.3 %all_to_all.33.second_ref = f32[8,16,128]{2,1,0:T(8,128)S(1)} all-to-all(f32[8,16,128]{2,1,0:T(8,128)S(1)} %get-tuple-element.21), channel_id=1, replica_groups=mesh['sky'=4,'exp'=8] {'exp'}, dimensions={0} | all-to-all | bytes 131072 | tf_op jit(solution)/shard_map/all_to_all | solution.py:308
  55.9 1.3 %shard_map.72 = (f32[32,1152]{1,0:T(8,128)S(1)}, f32[96,128]{1,0:T(8,128)S(1)}, f32[8,128]{1,0:T(8,128)S(1)}) custom-call(f32[8,16,128]{2,1,0:T(8,128)S(1)} %all_to_all.31.values_ref.first_ref, f32[8,16,128]{2,1,0:T(8,128)S(1)} %all_to_all.33.second_ref, s32[1,1,8,1024]{3,2,1,0:T(8,128)S(1)} %copy-done.1, f32[8,1024]{1,0:T(8,128)S(1)} %copy-done.2, ...), custom_call_target="tpu_custom_call" | custom-call | flops 2000000000 | bytes 1048576 | tf_op jit(solution)/shard_map/pallas_call | solution.py:334
  57.1 0.2 copy.7
  57.3 10.0 %all_to_all.34 = f32[32,1,1152]{2,1,0:T(1,128)S(1)} all-to-all(f32[32,1,1152]{2,1,0:T(1,128)S(1)} %copy.7), channel_id=1, replica_groups=mesh['sky'=4,'exp'=8] {'sky','exp'}, dimensions={0} | all-to-all | bytes 294912 | tf_op jit(solution)/shard_map/all_to_all | solution.py:305
  67.3 3.5 %shard_map.73 = (f32[96,128]{1,0:T(8,128)}, f32[96,128]{1,0:T(8,128)}) custom-call(f32[32,1152]{1,0:T(8,128)S(1)} %bitcast.9, s32[32,1024]{1,0:T(8,128)S(1)} %get-tuple-element.19.all_ref, f32[96,128]{1,0:T(8,128)S(1)} %get-tuple-element.20.right_ref, f32[96,128]{1,0:T(8,128)S(1)} %get-tuple-element.22.image_ref, ...), custom_call_target="tpu_custom_call" | custom-call | flops 2000000000 | bytes 1048576 | tf_op jit(solution)/shard_map/pallas_call | solution.py:338
  (1 shorter events, 0.0 us)
Async XLA Ops:
  4.0 7.3 %copy-start = (s32[1,1,8,1024]{3,2,1,0:T(8,128)S(1)}, s32[1,1,8,1024]{3,2,1,0:T(8,128)}, u32[]{:S(2)}) copy-start(s32[1,1,8,1024]{3,2,1,0:T(8,128)} %zp_ref.1) | copy-start | bytes 98308
  4.0 15.5 %all-to-all-start = ((f32[32,8,128]{2,1,0:T(8,128)}), f32[32,8,128]{2,1,0:T(8,128)S(1)}, u32[]{:S(2)}, u32[]{:S(2)}) async-start(f32[32,8,128]{2,1,0:T(8,128)} %get-tuple-element.15), calls=%async_computation | async-start | bytes 262144 | tf_op jit(solution)/shard_map/all_to_all | solution.py:305
  11.3 5.1 %collective-permute-start.2 = (s32[1,1,8,1024]{3,2,1,0:T(8,128)S(1)}, s32[1,1,8,1024]{3,2,1,0:T(8,128)S(1)}, u32[]{:S(2)}, u32[]{:S(2)}) collective-permute-start(s32[1,1,8,1024]{3,2,1,0:T(8,128)S(1)} %copy-done), channel_id=1, source_target_pairs={{0,24},{8,16},{16,8},{24,0},{1,25},{9,17},{17,9},{25,1},{2,26},{10... | collective-permute-start | bytes 98312 | tf_op jit(solution)/shard_map/ppermute | solution.py:310
  14.0 4.1 %collective-permute-start.1 = (s32[1,1,8,1024]{3,2,1,0:T(8,128)S(1)}, s32[1,1,8,1024]{3,2,1,0:T(8,128)S(1)}, u32[]{:S(2)}, u32[]{:S(2)}) collective-permute-start(s32[1,1,8,1024]{3,2,1,0:T(8,128)S(1)} %copy-done), channel_id=1, source_target_pairs={{0,16},{8,24},{16,0},{24,8},{1,17},{9,25},{17,1},{25,9},{2,18},{10... | collective-permute-start | bytes 98312 | tf_op jit(solution)/shard_map/ppermute | solution.py:310
  14.6 4.0 %collective-permute-start = (s32[1,1,8,1024]{3,2,1,0:T(8,128)S(1)}, s32[1,1,8,1024]{3,2,1,0:T(8,128)S(1)}, u32[]{:S(2)}, u32[]{:S(2)}) collective-permute-start(s32[1,1,8,1024]{3,2,1,0:T(8,128)S(1)} %copy-done), channel_id=1, source_target_pairs={{0,8},{8,0},{16,24},{24,16},{1,9},{9,1},{17,25},{25,17},{2,10},{10... | collective-permute-start | bytes 98312 | tf_op jit(solution)/shard_map/ppermute | solution.py:310
  23.1 9.5 %copy-start.1 = (s32[1,1,8,1024]{3,2,1,0:T(8,128)S(1)}, s32[1,1,8,1024]{3,2,1,0:T(8,128)}, u32[]{:S(2)}) copy-start(s32[1,1,8,1024]{3,2,1,0:T(8,128)} %star_ref.3) | copy-start | bytes 98308
  23.1 9.5 %copy-start.2 = (f32[8,1024]{1,0:T(8,128)S(1)}, f32[8,1024]{1,0:T(8,128)}, u32[]{:S(2)}) copy-start(f32[8,1024]{1,0:T(8,128)} %get-tuple-element.17.live_ref) | copy-start | bytes 98308
  23.1 9.5 %copy-start.3 = (f32[32,128]{1,0:T(8,128)S(1)}, f32[32,128]{1,0:T(8,128)}, u32[]{:S(2)}) copy-start(f32[32,128]{1,0:T(8,128)} %get-tuple-element.18.scale_ref) | copy-start | bytes 49156

commit v4 on v3

--- a/solution.py
+++ b/solution.py
@@ -103,13 +103,13 @@
     lax.fori_loop(0, n_rows // SUB, block, 0)
 
 
-def first_terms(n_sky, count_ref, weight_from, magnitude_from, star_from, terms_ref, live_ref, scale_ref,
-                weight_ref, magnitude_ref, star_ref, moment_ref, sums_ref, mean_ref, arrival):
+def first_terms(n_sky, count_from, weight_from, magnitude_from, star_from, terms_ref, live_ref, scale_ref,
+                count_ref, weight_ref, magnitude_ref, star_ref, moment_ref, sums_ref, mean_ref, arrival):
     n_rows, cap = weight_from.shape[2:]
     copies = [
         pltpu.make_async_copy(source, target, arrival.at[n])
         for n, (source, target) in enumerate(
-            [(weight_from, weight_ref), (magnitude_from, magnitude_ref), (star_from, star_ref)])
+            [(count_from, count_ref), (weight_from, weight_ref), (magnitude_from, magnitude_ref), (star_from, star_ref)])
     ]
     for copy in copies:
         copy.start()
@@ -313,9 +313,9 @@
     sent, live, scale = pl.pallas_call(
         functools.partial(first_terms, n_sky),
         out_shape=[jax.ShapeDtypeStruct(shape, f32) for shape in (terms, slots, star)],
-        in_specs=[smem, anywhere, anywhere, anywhere],
-        scratch_shapes=[pltpu.VMEM(whole, f32), pltpu.VMEM(whole, f32), pltpu.VMEM(whole, jnp.int32),
-                        pltpu.VMEM(slots, f32), pltpu.VMEM(star, f32), pltpu.VMEM(star, f32), pltpu.SemaphoreType.DMA((3,))],
+        in_specs=[anywhere] * 4,
+        scratch_shapes=[pltpu.SMEM((1, 1, n_exp), jnp.int32), pltpu.VMEM(whole, f32), pltpu.VMEM(whole, f32), pltpu.VMEM(whole, jnp.int32),
+                        pltpu.VMEM(slots, f32), pltpu.VMEM(star, f32), pltpu.VMEM(star, f32), pltpu.SemaphoreType.DMA((4,))],
         compiler_params=pltpu.CompilerParams(vmem_limit_bytes=58 << 20),
         cost_estimate=pl.CostEstimate(flops=2_000_000_000, bytes_accessed=1 << 20, transcendentals=0),
     )(peer_count, obs_weight, magnitude, star_id)

time: 71.3 us -> 70.7 us (level)
  no operation moved by 1% of the time
where the time goes in v4:
time: 70.7 us; the launch traced here: 70.2 us
  blocking collectives  38 us (54%)
  Pallas kernels  15.8 us (22%)
  starting transfers between devices  10.9 us (15%)
  waiting for transfers between devices  4.61 us (7%)
  between operations  0.73 us (1%)
    all_to_all x2, blocking collectives, to_owners(): lax.all_to_all(x, ('sky', 'exp'), split_axis=0, concat_axis=0, tiled=True)  20.2 us
    all_to_all x2, blocking collectives, to_sources(): return lax.all_to_all(x, 'exp', split_axis=0, concat_axis=0, tiled=True)  17.8 us
    all_to_all x1, starting transfers between devices, to_owners(): lax.all_to_all(x, ('sky', 'exp'), split_axis=0, concat_axis=0, tiled=True)  7.31 us
    ppermute x3, waiting for transfers between devices, body(): lax.ppermute(zp_index, 'sky', [(i, i ^ d) for i in range(n_sky)])  3.73 us
    pallas_call x1, Pallas kernels, body(): call(second_owner, [picks, tall])(arrived, zp_all, right, zp_index)  3.65 us
    pallas_call x1, Pallas kernels, body(): pl.pallas_call(functools.partial(first_owner, n_sky), out_shape=[jax.Shap...  3.63 us
    ppermute x3, starting transfers between devices, body(): lax.ppermute(zp_index, 'sky', [(i, i ^ d) for i in range(n_sky)])  3.55 us
    pallas_call x1, Pallas kernels, body(): call(last_owner, [tall, tall], [tall])  3.51 us
  transfers between devices with their start and end apart: 4, of which 4 were waited for; matrix products, arithmetic and copies ran while one was open for 0% of the time, Pallas kernels for 0%

profile of v4, /device:TPU:0, one launch (start us, length us, event | category | flops | bytes accessed | tf_op | source)
XLA Modules:
  0.0 70.2 jit_solution(3205316554122255889)
XLA Ops:
  0.6 2.7 %shard_map.68 = (f32[32,8,128]{2,1,0:T(8,128)}, f32[8,1024]{1,0:T(8,128)}, f32[32,128]{1,0:T(8,128)}) custom-call(s32[1,1,8]{2,1,0:T(1,128)} %count_from.1, f32[1,1,8,1024]{3,2,1,0:T(8,128)} %weight_from.1, f32[1,1,8,1024]{3,2,1,0:T(8,128)} %magnitude_from.1, s32[1,1,8,1024]{3,2,1,0:T(8,128)} %star_ref.3), custom_call_target="tpu_custom_call" | custom-call | flops 2000000000 | bytes 1048576 | tf_op jit(solution)/shard_map/pallas_call | solution.py:313
  3.3 0.0 copy-start
  3.3 7.3 %all-to-all-start = ((f32[32,8,128]{2,1,0:T(8,128)}), f32[32,8,128]{2,1,0:T(8,128)S(1)}, u32[]{:S(2)}, u32[]{:S(2)}) async-start(f32[32,8,128]{2,1,0:T(8,128)} %get-tuple-element.15), calls=%async_computation | async-start | bytes 262144 | tf_op jit(solution)/shard_map/all_to_all | solution.py:305
  10.6 0.0 copy-done
  10.7 2.7 %collective-permute-start.2 = (s32[1,1,8,1024]{3,2,1,0:T(8,128)S(1)}, s32[1,1,8,1024]{3,2,1,0:T(8,128)S(1)}, u32[]{:S(2)}, u32[]{:S(2)}) collective-permute-start(s32[1,1,8,1024]{3,2,1,0:T(8,128)S(1)} %copy-done), channel_id=1, source_target_pairs={{0,24},{8,16},{16,8},{24,0},{1,25},{9,17},{17,9},{25,1},{2,26},{10... | collective-permute-start | bytes 98312 | tf_op jit(solution)/shard_map/ppermute | solution.py:310
  13.4 0.6 collective-permute-start.1
  13.9 0.3 collective-permute-start
  14.2 1.5 %collective-permute-done.2.refs_3_ = s32[1,1,8,1024]{3,2,1,0:T(8,128)S(1)} collective-permute-done((s32[1,1,8,1024]{3,2,1,0:T(8,128)S(1)}, s32[1,1,8,1024]{3,2,1,0:T(8,128)S(1)}, u32[]{:S(2)}, u32[]{:S(2)}) %collective-permute-start.2) | collective-permute-done | bytes 32800 | tf_op jit(solution)/shard_map/ppermute | solution.py:310
  15.7 1.8 %collective-permute-done.1.refs_2_ = s32[1,1,8,1024]{3,2,1,0:T(8,128)S(1)} collective-permute-done((s32[1,1,8,1024]{3,2,1,0:T(8,128)S(1)}, s32[1,1,8,1024]{3,2,1,0:T(8,128)S(1)}, u32[]{:S(2)}, u32[]{:S(2)}) %collective-permute-start.1) | collective-permute-done | bytes 32800 | tf_op jit(solution)/shard_map/ppermute | solution.py:310
  17.5 0.4 collective-permute-done.refs_1_
  17.9 0.9 %all-to-all-done.arrived_ref = f32[32,8,128]{2,1,0:T(8,128)S(1)} async-done(((f32[32,8,128]{2,1,0:T(8,128)}), f32[32,8,128]{2,1,0:T(8,128)S(1)}, u32[]{:S(2)}, u32[]{:S(2)}) %all-to-all-start) | async-done | bytes 131104 | tf_op jit(solution)/shard_map/all_to_all | solution.py:305
  18.8 3.6 %shard_map.69 = (f32[8,16,128]{2,1,0:T(8,128)S(1)}, s32[32,1024]{1,0:T(8,128)S(1)}, f32[96,128]{1,0:T(8,128)S(1)}) custom-call(s32[1]{0:T(128)} %bitcast.me_ref, f32[32,8,128]{2,1,0:T(8,128)S(1)} %all-to-all-done.arrived_ref, s32[1,1,8,1024]{3,2,1,0:T(8,128)S(1)} %copy-done, s32[1,1,8,1024]{3,2,1,0:T(8,128)S(1)} %collective-permute-done.refs_1_, ...), custom_call_target="tpu_custom_call" | custom-call | tf_op jit(solution)/shard_map/pallas_call | solution.py:323
  22.5 0.0 copy-start.1
  22.5 0.0 copy-start.2
  22.5 0.0 copy-start.3
  22.5 9.5 %all_to_all.31.values_ref.first_ref = f32[8,16,128]{2,1,0:T(8,128)S(1)} all-to-all(f32[8,16,128]{2,1,0:T(8,128)S(1)} %get-tuple-element.16), channel_id=1, replica_groups=mesh['sky'=4,'exp'=8] {'exp'}, dimensions={0} | all-to-all | bytes 131072 | tf_op jit(solution)/shard_map/all_to_all | solution.py:308
  32.0 0.0 copy-done.1
  32.0 0.0 copy-done.2
  32.0 0.0 copy-done.3
  32.0 1.1 %shard_map.70 = f32[32,8,128]{2,1,0:T(8,128)S(1)} custom-call(f32[8,16,128]{2,1,0:T(8,128)S(1)} %all_to_all.31.values_ref.first_ref, s32[1,1,8,1024]{3,2,1,0:T(8,128)S(1)} %copy-done.1, f32[8,1024]{1,0:T(8,128)S(1)} %copy-done.2, f32[32,128]{1,0:T(8,128)S(1)} %copy-done.3), custom_call_target="tpu_custom_call" | custom-call | flops 2000000000 | bytes 1048576 | tf_op jit(solution)/shard_map/pallas_call | solution.py:330
  33.1 10.2 %all_to_all.32.arrived_ref = f32[32,8,128]{2,1,0:T(8,128)S(1)} all-to-all(f32[32,8,128]{2,1,0:T(8,128)S(1)} %shard_map.70), channel_id=1, replica_groups=mesh['sky'=4,'exp'=8] {'sky','exp'}, dimensions={0} | all-to-all | bytes 262144 | tf_op jit(solution)/shard_map/all_to_all | solution.py:305
  43.3 3.6 %shard_map.71 = (f32[8,16,128]{2,1,0:T(8,128)S(1)}, f32[96,128]{1,0:T(8,128)S(1)}) custom-call(f32[32,8,128]{2,1,0:T(8,128)S(1)} %all_to_all.32.arrived_ref, s32[32,1024]{1,0:T(8,128)S(1)} %get-tuple-element.19.all_ref, f32[96,128]{1,0:T(8,128)S(1)} %get-tuple-element.20.right_ref, s32[1,1,8,1024]{3,2,1,0:T(8,128)S(1)} %copy-done), custom_call_target="tpu_custom_call" | custom-call | flops 2000000000 | bytes 1048576 | tf_op jit(solution)/shard_map/pallas_call | solution.py:332
  46.9 8.3 %all_to_all.33.second_ref = f32[8,16,128]{2,1,0:T(8,128)S(1)} all-to-all(f32[8,16,128]{2,1,0:T(8,128)S(1)} %get-tuple-element.21), channel_id=1, replica_groups=mesh['sky'=4,'exp'=8] {'exp'}, dimensions={0} | all-to-all | bytes 131072 | tf_op jit(solution)/shard_map/all_to_all | solution.py:308
  55.2 1.3 %shard_map.72 = (f32[32,1152]{1,0:T(8,128)S(1)}, f32[96,128]{1,0:T(8,128)S(1)}, f32[8,128]{1,0:T(8,128)S(1)}) custom-call(f32[8,16,128]{2,1,0:T(8,128)S(1)} %all_to_all.31.values_ref.first_ref, f32[8,16,128]{2,1,0:T(8,128)S(1)} %all_to_all.33.second_ref, s32[1,1,8,1024]{3,2,1,0:T(8,128)S(1)} %copy-done.1, f32[8,1024]{1,0:T(8,128)S(1)} %copy-done.2, ...), custom_call_target="tpu_custom_call" | custom-call | flops 2000000000 | bytes 1048576 | tf_op jit(solution)/shard_map/pallas_call | solution.py:334
  56.5 0.2 copy.7
  56.7 10.0 %all_to_all.34 = f32[32,1,1152]{2,1,0:T(1,128)S(1)} all-to-all(f32[32,1,1152]{2,1,0:T(1,128)S(1)} %copy.7), channel_id=1, replica_groups=mesh['sky'=4,'exp'=8] {'sky','exp'}, dimensions={0} | all-to-all | bytes 294912 | tf_op jit(solution)/shard_map/all_to_all | solution.py:305
  66.7 3.5 %shard_map.73 = (f32[96,128]{1,0:T(8,128)}, f32[96,128]{1,0:T(8,128)}) custom-call(f32[32,1152]{1,0:T(8,128)S(1)} %bitcast.9, s32[32,1024]{1,0:T(8,128)S(1)} %get-tuple-element.19.all_ref, f32[96,128]{1,0:T(8,128)S(1)} %get-tuple-element.20.right_ref, f32[96,128]{1,0:T(8,128)S(1)} %get-tuple-element.22.image_ref, ...), custom_call_target="tpu_custom_call" | custom-call | flops 2000000000 | bytes 1048576 | tf_op jit(solution)/shard_map/pallas_call | solution.py:338
  (1 shorter events, 0.0 us)
Async XLA Ops:
  3.3 7.3 %copy-start = (s32[1,1,8,1024]{3,2,1,0:T(8,128)S(1)}, s32[1,1,8,1024]{3,2,1,0:T(8,128)}, u32[]{:S(2)}) copy-start(s32[1,1,8,1024]{3,2,1,0:T(8,128)} %zp_ref.1) | copy-start | bytes 98308
  3.3 15.5 %all-to-all-start = ((f32[32,8,128]{2,1,0:T(8,128)}), f32[32,8,128]{2,1,0:T(8,128)S(1)}, u32[]{:S(2)}, u32[]{:S(2)}) async-start(f32[32,8,128]{2,1,0:T(8,128)} %get-tuple-element.15), calls=%async_computation | async-start | bytes 262144 | tf_op jit(solution)/shard_map/all_to_all | solution.py:305
  10.7 5.1 %collective-permute-start.2 = (s32[1,1,8,1024]{3,2,1,0:T(8,128)S(1)}, s32[1,1,8,1024]{3,2,1,0:T(8,128)S(1)}, u32[]{:S(2)}, u32[]{:S(2)}) collective-permute-start(s32[1,1,8,1024]{3,2,1,0:T(8,128)S(1)} %copy-done), channel_id=1, source_target_pairs={{0,24},{8,16},{16,8},{24,0},{1,25},{9,17},{17,9},{25,1},{2,26},{10... | collective-permute-start | bytes 98312 | tf_op jit(solution)/shard_map/ppermute | solution.py:310
  13.4 4.1 %collective-permute-start.1 = (s32[1,1,8,1024]{3,2,1,0:T(8,128)S(1)}, s32[1,1,8,1024]{3,2,1,0:T(8,128)S(1)}, u32[]{:S(2)}, u32[]{:S(2)}) collective-permute-start(s32[1,1,8,1024]{3,2,1,0:T(8,128)S(1)} %copy-done), channel_id=1, source_target_pairs={{0,16},{8,24},{16,0},{24,8},{1,17},{9,25},{17,1},{25,9},{2,18},{10... | collective-permute-start | bytes 98312 | tf_op jit(solution)/shard_map/ppermute | solution.py:310
  13.9 4.0 %collective-permute-start = (s32[1,1,8,1024]{3,2,1,0:T(8,128)S(1)}, s32[1,1,8,1024]{3,2,1,0:T(8,128)S(1)}, u32[]{:S(2)}, u32[]{:S(2)}) collective-permute-start(s32[1,1,8,1024]{3,2,1,0:T(8,128)S(1)} %copy-done), channel_id=1, source_target_pairs={{0,8},{8,0},{16,24},{24,16},{1,9},{9,1},{17,25},{25,17},{2,10},{10... | collective-permute-start | bytes 98312 | tf_op jit(solution)/shard_map/ppermute | solution.py:310
  22.5 9.5 %copy-start.1 = (s32[1,1,8,1024]{3,2,1,0:T(8,128)S(1)}, s32[1,1,8,1024]{3,2,1,0:T(8,128)}, u32[]{:S(2)}) copy-start(s32[1,1,8,1024]{3,2,1,0:T(8,128)} %star_ref.3) | copy-start | bytes 98308
  22.5 9.5 %copy-start.2 = (f32[8,1024]{1,0:T(8,128)S(1)}, f32[8,1024]{1,0:T(8,128)}, u32[]{:S(2)}) copy-start(f32[8,1024]{1,0:T(8,128)} %get-tuple-element.17.live_ref) | copy-start | bytes 98308
  22.5 9.5 %copy-start.3 = (f32[32,128]{1,0:T(8,128)S(1)}, f32[32,128]{1,0:T(8,128)}, u32[]{:S(2)}) copy-start(f32[32,128]{1,0:T(8,128)} %get-tuple-element.18.scale_ref) | copy-start | bytes 49156

commit v5 on v4

--- a/solution.py
+++ b/solution.py
@@ -163,19 +163,19 @@
     lax.fori_loop(0, n_rows // step, block, 0)
 
 
-def send_picks(zp_ref, table_ref, out_ref, scalar):
+def send_picks(zp_ref, table_ref, out_ref, extra=0):
     n_rows, cap = zp_ref.shape[2:]
+    block = cap // LANES + extra
     for g in range(n_rows // SUB):
         rows = slice(g * SUB, (g + 1) * SUB)
 
         def one(a, carry, rows=rows):
             lanes = pl.ds(pl.multiple_of(a * LANES, LANES), LANES)
             index = zp_ref[0, 0, rows, lanes]
-            out_ref[rows, pl.ds(a, 1), :] = pick(table_ref, index, ZP_ROWS).reshape(SUB, 1, LANES)
+            out_ref[pl.ds(rows.start * block + a, SUB, stride=block), :] = pick(table_ref, index, ZP_ROWS)
             return carry
 
         lax.fori_loop(0, cap // LANES, one, 0, unroll=4)
-    out_ref[:, cap // LANES, :] = jnp.broadcast_to(scalar, (n_rows, LANES))
 
 
 def first_owner(n_sky, me_ref, arrived_ref, *refs):
@@ -189,8 +189,7 @@
         return arrived_ref[pl.ds(first + r, 1), a, :]
 
     owner_sums(all_ref, arrived, n_sky * n_rows, cap, right_ref, 32)
-    right = right_ref[...]
-    send_picks(zp_refs[0], right_ref, sent_ref, whole_sum(right * right))
+    send_picks(zp_refs[0], right_ref, sent_ref)
 
 
 def star_terms(n_sky, star_ref, live_ref, scale_ref, slot_ref, product_ref, sums_ref, mean_ref, emit):
@@ -231,15 +230,20 @@
     owner_sums(all_ref, arrived, all_ref.shape[0], cap, image_ref, 32)
     right = right_ref[...]
     image_ref[...] = image_ref[...] + ridge * right
-    send_picks(zp_ref, image_ref, sent_ref, whole_sum(right * image_ref[...]))
+    send_picks(zp_ref, image_ref, sent_ref, 1)
+    lane = lax.broadcasted_iota(jnp.int32, (1, LANES), 1)
+    both = jnp.where(lane < LANES // 2, whole_sum(right * right), whole_sum(right * image_ref[...]))
+    block = cap // LANES + 1
+    sent_ref[pl.ds(block - 1, n_rows, stride=block), :] = jnp.broadcast_to(both, (n_rows, LANES))
 
 
 def third_terms(n_sky, first_ref, second_ref, star_ref, live_ref, scale_ref, right_ref, image_ref,
                 terms_ref, residual_ref, scalar_ref, slot_ref, product_ref, sums_ref, mean_ref):
     n_rows, cap = live_ref.shape
     extra = cap // LANES
-    norm = jnp.sum(first_ref[:, extra, :], axis=0, keepdims=True)
-    product = jnp.sum(second_ref[:, extra, :], axis=0, keepdims=True)
+    sums = jnp.sum(second_ref[:, cap:cap + LANES], axis=0, keepdims=True)
+    norm = jnp.broadcast_to(sums[:, 0:1], (1, LANES))
+    product = jnp.broadcast_to(sums[:, LANES // 2:LANES // 2 + 1], (1, LANES))
     alpha = norm / product
     scalar_ref[0:1, :] = norm
     scalar_ref[1:2, :] = alpha
@@ -248,16 +252,16 @@
     square = whole_sum(residual * residual)
     for g, a in tiles(n_rows, cap):
         rows = slice(g * SUB, (g + 1) * SUB)
-        slot_ref[at(g, a)] = first_ref[rows, a, :] - alpha * second_ref[rows, a, :]
+        slot_ref[at(g, a)] = first_ref[rows, a, :] - alpha * second_ref[at(g, a)]
 
     def emit(g, a, term):
         for i in range(n_sky):
-            terms_ref[i * n_rows + g * SUB:i * n_rows + (g + 1) * SUB, a * LANES:(a + 1) * LANES] = term
+            terms_ref[pl.ds((i * n_rows + g * SUB) * (extra + 1) + a, SUB, stride=extra + 1), :] = term
 
     along = star_terms(n_sky, star_ref, live_ref, scale_ref, slot_ref, product_ref, sums_ref, mean_ref, emit)
     lane = lax.broadcasted_iota(jnp.int32, (1, LANES), 1)
     both = jnp.where(lane < LANES // 2, along, square * (1.0 / n_sky))
-    terms_ref[:, cap:cap + LANES] = jnp.broadcast_to(both, (n_sky * n_rows, LANES))
+    terms_ref[pl.ds(extra, n_sky * n_rows, stride=extra + 1), :] = jnp.broadcast_to(both, (n_sky * n_rows, LANES))
 
 
 def last_owner(arrived_ref, all_ref, right_ref, image_ref, residual_ref, scalar_ref, points_ref, left_ref, total_ref):
@@ -296,7 +300,7 @@
     cap = obs_weight.shape[3]
     tall, star, slots = (ZP_ROWS, LANES), (STAR_ROWS, LANES), (n_exp, cap)
     terms = (n_sky * n_exp, cap // LANES, LANES)
-    picks = (n_exp, 2 * SUB, LANES)
+    picks = (n_exp * (cap // LANES + 1), LANES)
     vmem = pl.BlockSpec(memory_space=pltpu.VMEM)
     smem = pl.BlockSpec(memory_space=pltpu.SMEM)
     me = jnp.reshape(lax.axis_index("sky"), (1,)).astype(jnp.int32)
@@ -322,19 +326,19 @@
     arrived = to_owners(sent)
     sent, zp_all, right = pl.pallas_call(
         functools.partial(first_owner, n_sky),
-        out_shape=[jax.ShapeDtypeStruct(picks, f32), jax.ShapeDtypeStruct((n_sky * n_exp, cap), jnp.int32), jax.ShapeDtypeStruct(tall, f32)],
+        out_shape=[jax.ShapeDtypeStruct((n_exp * (cap // LANES), LANES), f32), jax.ShapeDtypeStruct((n_sky * n_exp, cap), jnp.int32), jax.ShapeDtypeStruct(tall, f32)],
         in_specs=[smem] + [vmem] * (n_sky + 1),
         compiler_params=pltpu.CompilerParams(vmem_limit_bytes=40 << 20),
     )(me, arrived, *zp)
-    first = to_sources(sent)
+    first = to_sources(sent.reshape(n_exp, cap // LANES, LANES))
     (sent,) = call(functools.partial(second_terms, n_sky), [terms], [slots, slots, star, star])(first, star_id, live, scale)
     arrived = to_owners(sent)
     sent, image = call(second_owner, [picks, tall])(arrived, zp_all, right, zp_index)
-    second = to_sources(sent)
+    second = to_sources(sent.reshape(n_exp, cap + LANES))
     sent, residual, scalars = call(
-        functools.partial(third_terms, n_sky), [(n_sky * n_exp, cap + LANES), tall, (SUB, LANES)], [slots, slots, star, star]
+        functools.partial(third_terms, n_sky), [(n_sky * n_exp * (cap // LANES + 1), LANES), tall, (SUB, LANES)], [slots, slots, star, star]
     )(first, second, star_id, live, scale, right, image)
-    arrived = to_owners(sent)
+    arrived = to_owners(sent.reshape(n_sky * n_exp, cap + LANES))
     points, left = call(last_owner, [tall, tall], [tall])(arrived, zp_all, right, image, residual, scalars)
     return points.reshape(-1)[:ZP_DEV], left.reshape(-1)[:ZP_DEV]
 

time: 70.7 us -> 69.7 us (0.986)
  no operation moved by 1% of the time
where the time goes in v5:
time: 69.7 us; the launch traced here: 69.3 us
  blocking collectives  37.3 us (54%)
  Pallas kernels  15.8 us (23%)
  starting transfers between devices  10.9 us (16%)
  waiting for transfers between devices  4.61 us (7%)
  between operations  0.72 us (1%)
    all_to_all x2, blocking collectives, to_owners(): lax.all_to_all(x, ('sky', 'exp'), split_axis=0, concat_axis=0, tiled=True)  19.9 us
    all_to_all x2, blocking collectives, to_sources(): return lax.all_to_all(x, 'exp', split_axis=0, concat_axis=0, tiled=True)  17.3 us
    all_to_all x1, starting transfers between devices, to_owners(): lax.all_to_all(x, ('sky', 'exp'), split_axis=0, concat_axis=0, tiled=True)  7.31 us
    ppermute x3, waiting for transfers between devices, body(): lax.ppermute(zp_index, 'sky', [(i, i ^ d) for i in range(n_sky)])  3.73 us
    pallas_call x1, Pallas kernels, body(): call(second_owner, [picks, tall])(arrived, zp_all, right, zp_index)  3.63 us
    ppermute x3, starting transfers between devices, body(): lax.ppermute(zp_index, 'sky', [(i, i ^ d) for i in range(n_sky)])  3.55 us
    pallas_call x1, Pallas kernels, body(): pl.pallas_call(functools.partial(first_owner, n_sky), out_shape=[jax.Shap...  3.53 us
    pallas_call x1, Pallas kernels, body(): call(last_owner, [tall, tall], [tall])  3.51 us
  transfers between devices with their start and end apart: 4, of which 4 were waited for; matrix products, arithmetic and copies ran while one was open for 0% of the time, Pallas kernels for 0%

profile of v5, /device:TPU:0, one launch (start us, length us, event | category | flops | bytes accessed | tf_op | source)
XLA Modules:
  0.0 69.3 jit_solution(6198449051034345371)
XLA Ops:
  0.6 2.7 %shard_map.68 = (f32[32,8,128]{2,1,0:T(8,128)}, f32[8,1024]{1,0:T(8,128)}, f32[32,128]{1,0:T(8,128)}) custom-call(s32[1,1,8]{2,1,0:T(1,128)} %count_from.1, f32[1,1,8,1024]{3,2,1,0:T(8,128)} %weight_from.1, f32[1,1,8,1024]{3,2,1,0:T(8,128)} %magnitude_from.1, s32[1,1,8,1024]{3,2,1,0:T(8,128)} %star_ref.3), custom_call_target="tpu_custom_call" | custom-call | flops 2000000000 | bytes 1048576 | tf_op jit(solution)/shard_map/pallas_call | solution.py:317
  3.3 0.0 copy-start
  3.3 7.3 %all-to-all-start = ((f32[32,8,128]{2,1,0:T(8,128)}), f32[32,8,128]{2,1,0:T(8,128)S(1)}, u32[]{:S(2)}, u32[]{:S(2)}) async-start(f32[32,8,128]{2,1,0:T(8,128)} %get-tuple-element.15), calls=%async_computation | async-start | bytes 262144 | tf_op jit(solution)/shard_map/all_to_all | solution.py:309
  10.6 0.0 copy-done
  10.7 2.7 %collective-permute-start.2 = (s32[1,1,8,1024]{3,2,1,0:T(8,128)S(1)}, s32[1,1,8,1024]{3,2,1,0:T(8,128)S(1)}, u32[]{:S(2)}, u32[]{:S(2)}) collective-permute-start(s32[1,1,8,1024]{3,2,1,0:T(8,128)S(1)} %copy-done), channel_id=1, source_target_pairs={{0,24},{8,16},{16,8},{24,0},{1,25},{9,17},{17,9},{25,1},{2,26},{10... | collective-permute-start | bytes 98312 | tf_op jit(solution)/shard_map/ppermute | solution.py:314
  13.4 0.6 collective-permute-start.1
  13.9 0.3 collective-permute-start
  14.2 1.5 %collective-permute-done.2.refs_3_ = s32[1,1,8,1024]{3,2,1,0:T(8,128)S(1)} collective-permute-done((s32[1,1,8,1024]{3,2,1,0:T(8,128)S(1)}, s32[1,1,8,1024]{3,2,1,0:T(8,128)S(1)}, u32[]{:S(2)}, u32[]{:S(2)}) %collective-permute-start.2) | collective-permute-done | bytes 32800 | tf_op jit(solution)/shard_map/ppermute | solution.py:314
  15.7 1.8 %collective-permute-done.1.refs_2_ = s32[1,1,8,1024]{3,2,1,0:T(8,128)S(1)} collective-permute-done((s32[1,1,8,1024]{3,2,1,0:T(8,128)S(1)}, s32[1,1,8,1024]{3,2,1,0:T(8,128)S(1)}, u32[]{:S(2)}, u32[]{:S(2)}) %collective-permute-start.1) | collective-permute-done | bytes 32800 | tf_op jit(solution)/shard_map/ppermute | solution.py:314
  17.5 0.4 collective-permute-done.refs_1_
  17.9 0.9 %all-to-all-done.arrived_ref = f32[32,8,128]{2,1,0:T(8,128)S(1)} async-done(((f32[32,8,128]{2,1,0:T(8,128)}), f32[32,8,128]{2,1,0:T(8,128)S(1)}, u32[]{:S(2)}, u32[]{:S(2)}) %all-to-all-start) | async-done | bytes 131104 | tf_op jit(solution)/shard_map/all_to_all | solution.py:309
  18.8 0.0 copy-start.3
  18.8 3.5 %shard_map.69 = (f32[64,128]{1,0:T(8,128)S(1)}, s32[32,1024]{1,0:T(8,128)S(1)}, f32[96,128]{1,0:T(8,128)S(1)}) custom-call(s32[1]{0:T(128)} %bitcast.me_ref, f32[32,8,128]{2,1,0:T(8,128)S(1)} %all-to-all-done.arrived_ref, s32[1,1,8,1024]{3,2,1,0:T(8,128)S(1)} %copy-done, s32[1,1,8,1024]{3,2,1,0:T(8,128)S(1)} %collective-permute-done.refs_1_, ...), custom_call_target="tpu_custom_call" | custom-call | tf_op jit(solution)/shard_map/pallas_call | solution.py:327
  22.4 0.0 copy-start.1
  22.4 0.0 copy-start.2
  22.4 9.2 %all_to_all.37.values_ref.first_ref = f32[8,8,128]{2,1,0:T(8,128)S(1)} all-to-all(f32[8,8,128]{2,1,0:T(8,128)S(1)} %bitcast.18), channel_id=1, replica_groups=mesh['sky'=4,'exp'=8] {'exp'}, dimensions={0} | all-to-all | bytes 65536 | tf_op jit(solution)/shard_map/all_to_all | solution.py:312
  31.6 0.0 copy-done.3
  31.6 0.0 copy-done.1
  31.6 0.0 copy-done.2
  31.6 1.1 %shard_map.70 = f32[32,8,128]{2,1,0:T(8,128)S(1)} custom-call(f32[8,8,128]{2,1,0:T(8,128)S(1)} %all_to_all.37.values_ref.first_ref, s32[1,1,8,1024]{3,2,1,0:T(8,128)S(1)} %copy-done.1, f32[8,1024]{1,0:T(8,128)S(1)} %copy-done.2, f32[32,128]{1,0:T(8,128)S(1)} %copy-done.3), custom_call_target="tpu_custom_call" | custom-call | flops 2000000000 | bytes 1048576 | tf_op jit(solution)/shard_map/pallas_call | solution.py:334
  32.7 9.9 %all_to_all.38.arrived_ref = f32[32,8,128]{2,1,0:T(8,128)S(1)} all-to-all(f32[32,8,128]{2,1,0:T(8,128)S(1)} %shard_map.70), channel_id=1, replica_groups=mesh['sky'=4,'exp'=8] {'sky','exp'}, dimensions={0} | all-to-all | bytes 262144 | tf_op jit(solution)/shard_map/all_to_all | solution.py:309
  42.6 3.6 %shard_map.71 = (f32[72,128]{1,0:T(8,128)S(1)}, f32[96,128]{1,0:T(8,128)S(1)}) custom-call(f32[32,8,128]{2,1,0:T(8,128)S(1)} %all_to_all.38.arrived_ref, s32[32,1024]{1,0:T(8,128)S(1)} %get-tuple-element.19.all_ref, f32[96,128]{1,0:T(8,128)S(1)} %get-tuple-element.20.right_ref, s32[1,1,8,1024]{3,2,1,0:T(8,128)S(1)} %copy-done), custom_call_target="tpu_custom_call" | custom-call | flops 2000000000 | bytes 1048576 | tf_op jit(solution)/shard_map/pallas_call | solution.py:336
  46.3 8.1 %all_to_all.39 = f32[8,1,1152]{2,1,0:T(1,128)S(1)} all-to-all(f32[8,1,1152]{2,1,0:T(1,128)S(1)} %bitcast.17), channel_id=1, replica_groups=mesh['sky'=4,'exp'=8] {'exp'}, dimensions={0} | all-to-all | bytes 73728 | tf_op jit(solution)/shard_map/all_to_all | solution.py:312
  54.4 1.3 %shard_map.72 = (f32[288,128]{1,0:T(8,128)S(1)}, f32[96,128]{1,0:T(8,128)S(1)}, f32[8,128]{1,0:T(8,128)S(1)}) custom-call(f32[8,8,128]{2,1,0:T(8,128)S(1)} %all_to_all.37.values_ref.first_ref, f32[8,1152]{1,0:T(8,128)S(1)} %bitcast.16, s32[1,1,8,1024]{3,2,1,0:T(8,128)S(1)} %copy-done.1, f32[8,1024]{1,0:T(8,128)S(1)} %copy-done.2, f32[32,128]{1,0:T(8,128)S(1)} %copy-done.3, ...), custom_call_target="tpu_custom_call" | custom-call | flops 2000000000 | bytes 1048576 | tf_op jit(solution)/shard_map/pallas_call | solution.py:338
  55.7 10.0 %all_to_all.40 = f32[32,1,1152]{2,1,0:T(1,128)S(1)} all-to-all(f32[32,1,1152]{2,1,0:T(1,128)S(1)} %bitcast.15), channel_id=1, replica_groups=mesh['sky'=4,'exp'=8] {'sky','exp'}, dimensions={0} | all-to-all | bytes 294912 | tf_op jit(solution)/shard_map/all_to_all | solution.py:309
  65.8 3.5 %shard_map.73 = (f32[96,128]{1,0:T(8,128)}, f32[96,128]{1,0:T(8,128)}) custom-call(f32[32,1152]{1,0:T(8,128)S(1)} %bitcast.14, s32[32,1024]{1,0:T(8,128)S(1)} %get-tuple-element.19.all_ref, f32[96,128]{1,0:T(8,128)S(1)} %get-tuple-element.20.right_ref, f32[96,128]{1,0:T(8,128)S(1)} %get-tuple-element.22.image_ref, ...), custom_call_target="tpu_custom_call" | custom-call | flops 2000000000 | bytes 1048576 | tf_op jit(solution)/shard_map/pallas_call | solution.py:342
  (2 shorter events, 0.0 us)
Async XLA Ops:
  3.3 7.3 %copy-start = (s32[1,1,8,1024]{3,2,1,0:T(8,128)S(1)}, s32[1,1,8,1024]{3,2,1,0:T(8,128)}, u32[]{:S(2)}) copy-start(s32[1,1,8,1024]{3,2,1,0:T(8,128)} %zp_ref.1) | copy-start | bytes 98308
  3.3 15.5 %all-to-all-start = ((f32[32,8,128]{2,1,0:T(8,128)}), f32[32,8,128]{2,1,0:T(8,128)S(1)}, u32[]{:S(2)}, u32[]{:S(2)}) async-start(f32[32,8,128]{2,1,0:T(8,128)} %get-tuple-element.15), calls=%async_computation | async-start | bytes 262144 | tf_op jit(solution)/shard_map/all_to_all | solution.py:309
  10.7 5.1 %collective-permute-start.2 = (s32[1,1,8,1024]{3,2,1,0:T(8,128)S(1)}, s32[1,1,8,1024]{3,2,1,0:T(8,128)S(1)}, u32[]{:S(2)}, u32[]{:S(2)}) collective-permute-start(s32[1,1,8,1024]{3,2,1,0:T(8,128)S(1)} %copy-done), channel_id=1, source_target_pairs={{0,24},{8,16},{16,8},{24,0},{1,25},{9,17},{17,9},{25,1},{2,26},{10... | collective-permute-start | bytes 98312 | tf_op jit(solution)/shard_map/ppermute | solution.py:314
  13.4 4.1 %collective-permute-start.1 = (s32[1,1,8,1024]{3,2,1,0:T(8,128)S(1)}, s32[1,1,8,1024]{3,2,1,0:T(8,128)S(1)}, u32[]{:S(2)}, u32[]{:S(2)}) collective-permute-start(s32[1,1,8,1024]{3,2,1,0:T(8,128)S(1)} %copy-done), channel_id=1, source_target_pairs={{0,16},{8,24},{16,0},{24,8},{1,17},{9,25},{17,1},{25,9},{2,18},{10... | collective-permute-start | bytes 98312 | tf_op jit(solution)/shard_map/ppermute | solution.py:314
  13.9 4.0 %collective-permute-start = (s32[1,1,8,1024]{3,2,1,0:T(8,128)S(1)}, s32[1,1,8,1024]{3,2,1,0:T(8,128)S(1)}, u32[]{:S(2)}, u32[]{:S(2)}) collective-permute-start(s32[1,1,8,1024]{3,2,1,0:T(8,128)S(1)} %copy-done), channel_id=1, source_target_pairs={{0,8},{8,0},{16,24},{24,16},{1,9},{9,1},{17,25},{25,17},{2,10},{10... | collective-permute-start | bytes 98312 | tf_op jit(solution)/shard_map/ppermute | solution.py:314
  18.8 12.8 %copy-start.3 = (f32[32,128]{1,0:T(8,128)S(1)}, f32[32,128]{1,0:T(8,128)}, u32[]{:S(2)}) copy-start(f32[32,128]{1,0:T(8,128)} %get-tuple-element.18.scale_ref) | copy-start | bytes 49156
  22.4 9.2 %copy-start.1 = (s32[1,1,8,1024]{3,2,1,0:T(8,128)S(1)}, s32[1,1,8,1024]{3,2,1,0:T(8,128)}, u32[]{:S(2)}) copy-start(s32[1,1,8,1024]{3,2,1,0:T(8,128)} %star_ref.3) | copy-start | bytes 98308
  22.4 9.2 %copy-start.2 = (f32[8,1024]{1,0:T(8,128)S(1)}, f32[8,1024]{1,0:T(8,128)}, u32[]{:S(2)}) copy-start(f32[8,1024]{1,0:T(8,128)} %get-tuple-element.17.live_ref) | copy-start | bytes 98308

commit v6 on v5

--- a/solution.py
+++ b/solution.py
@@ -178,17 +178,35 @@
         lax.fori_loop(0, cap // LANES, one, 0, unroll=4)
 
 
-def first_owner(n_sky, me_ref, arrived_ref, *refs):
-    zp_refs, (sent_ref, all_ref, right_ref) = refs[:n_sky], refs[n_sky:]
+def own_owner(me_ref, arrived_ref, zp_ref, part_ref):
+    n_rows, cap = zp_ref.shape[2:]
+    base = me_ref[0] * n_rows
+
+    def arrived(first, r, a):
+        return arrived_ref[pl.ds(base + first + r, 1), a, :]
+
+    owner_sums(zp_ref.at[0, 0], arrived, n_rows, cap, part_ref)
+
+
+def first_owner(n_sky, me_ref, arrived_ref, part_ref, *refs):
+    zp_refs, (sent_ref, all_ref, right_ref, parts_ref, one_ref) = refs[:n_sky], refs[n_sky:]
     n_rows, cap = zp_refs[0].shape[2:]
+    parts_ref[pl.ds(pl.multiple_of(me_ref[0] * ZP_ROWS, SUB), ZP_ROWS), :] = part_ref[...]
     for d in range(n_sky):
-        start = pl.multiple_of((me_ref[0] ^ d) * n_rows, SUB)
-        all_ref[pl.ds(start, n_rows), :] = zp_refs[d][0, 0]
-
-    def arrived(first, r, a):
-        return arrived_ref[pl.ds(first + r, 1), a, :]
-
-    owner_sums(all_ref, arrived, n_sky * n_rows, cap, right_ref, 32)
+        group = me_ref[0] ^ d
+        base = pl.multiple_of(group * n_rows, SUB)
+        all_ref[pl.ds(base, n_rows), :] = zp_refs[d][0, 0]
+        if d:
+
+            def arrived(first, r, a, base=base):
+                return arrived_ref[pl.ds(base + first + r, 1), a, :]
+
+            owner_sums(zp_refs[d].at[0, 0], arrived, n_rows, cap, one_ref)
+            parts_ref[pl.ds(pl.multiple_of(group * ZP_ROWS, SUB), ZP_ROWS), :] = one_ref[...]
+    right = parts_ref[0:ZP_ROWS, :]
+    for n in range(1, n_sky):
+        right = right + parts_ref[n * ZP_ROWS:(n + 1) * ZP_ROWS, :]
+    right_ref[...] = right
     send_picks(zp_refs[0], right_ref, sent_ref)
 
 
@@ -324,12 +342,14 @@
         cost_estimate=pl.CostEstimate(flops=2_000_000_000, bytes_accessed=1 << 20, transcendentals=0),
     )(peer_count, obs_weight, magnitude, star_id)
     arrived = to_owners(sent)
+    (part,) = call(own_owner, [tall], in_specs=[smem, vmem, vmem])(me, arrived, zp_index)
     sent, zp_all, right = pl.pallas_call(
         functools.partial(first_owner, n_sky),
         out_shape=[jax.ShapeDtypeStruct((n_exp * (cap // LANES), LANES), f32), jax.ShapeDtypeStruct((n_sky * n_exp, cap), jnp.int32), jax.ShapeDtypeStruct(tall, f32)],
-        in_specs=[smem] + [vmem] * (n_sky + 1),
+        in_specs=[smem] + [vmem] * (n_sky + 2),
+        scratch_shapes=[pltpu.VMEM((n_sky * ZP_ROWS, LANES), f32), pltpu.VMEM(tall, f32)],
         compiler_params=pltpu.CompilerParams(vmem_limit_bytes=40 << 20),
-    )(me, arrived, *zp)
+    )(me, arrived, part, *zp)
     first = to_sources(sent.reshape(n_exp, cap // LANES, LANES))
     (sent,) = call(functools.partial(second_terms, n_sky), [terms], [slots, slots, star, star])(first, star_id, live, scale)
     arrived = to_owners(sent)

time: 69.7 us -> 69.1 us (level)
  blocking collectives: 37.3 us -> 36.4 us
    all_to_all x1, waiting for transfers between devices: 0.88 us -> 4.61 us  [to_owners(): lax.all_to_all(x, ('sky', 'exp'), split_axis=0, concat_axis=0, tiled=True)]
    ppermute x3, waiting for transfers between devices: 3.73 us -> 0.01 us  [body(): lax.ppermute(zp_index, 'sky', [(i, i ^ d) for i in range(n_sky)])]
    all_to_all x2, blocking collectives: 17.3 us -> 16.5 us  [to_sources(): return lax.all_to_all(x, 'exp', split_axis=0, concat_axis=0, tiled=True)]
    pallas_call x0 -> x1, Pallas kernels: none -> 0.8 us  [body(): call(own_owner, [tall], in_specs=[smem, vmem, vmem])(me, arrived, zp_index)]
  transfers between devices with their start and end apart: 4 -> 4, of which waited for: 4 -> 1; matrix products, arithmetic and copies ran while one was open for 0% -> 0% of each run, Pallas kernels for 0% -> 1%
where the time goes in v6:
time: 69.1 us; the launch traced here: 68.7 us
  blocking collectives  36.4 us (53%)
  Pallas kernels  16 us (23%)
  starting transfers between devices  10.9 us (16%)
  waiting for transfers between devices  4.62 us (7%)
  between operations  0.75 us (1%)
    all_to_all x2, blocking collectives, to_owners(): lax.all_to_all(x, ('sky', 'exp'), split_axis=0, concat_axis=0, tiled=True)  19.9 us
    all_to_all x2, blocking collectives, to_sources(): return lax.all_to_all(x, 'exp', split_axis=0, concat_axis=0, tiled=True)  16.5 us
    all_to_all x1, starting transfers between devices, to_owners(): lax.all_to_all(x, ('sky', 'exp'), split_axis=0, concat_axis=0, tiled=True)  7.31 us
    all_to_all x1, waiting for transfers between devices, to_owners(): lax.all_to_all(x, ('sky', 'exp'), split_axis=0, concat_axis=0, tiled=True)  4.61 us
    pallas_call x1, Pallas kernels, body(): call(second_owner, [picks, tall])(arrived, zp_all, right, zp_index)  3.63 us
    ppermute x3, starting transfers between devices, body(): lax.ppermute(zp_index, 'sky', [(i, i ^ d) for i in range(n_sky)])  3.55 us
    pallas_call x1, Pallas kernels, body(): call(last_owner, [tall, tall], [tall])  3.51 us
    pallas_call x1, Pallas kernels, body(): pl.pallas_call(functools.partial(first_owner, n_sky), out_shape=[jax.Shap...  2.96 us
  transfers between devices with their start and end apart: 4, of which 1 were waited for; matrix products, arithmetic and copies ran while one was open for 0% of the time, Pallas kernels for 1%

profile of v6, /device:TPU:0, one launch (start us, length us, event | category | flops | bytes accessed | tf_op | source)
XLA Modules:
  0.0 68.7 jit_solution(2383066970058799207)
XLA Ops:
  0.6 2.7 %shard_map.68 = (f32[32,8,128]{2,1,0:T(8,128)}, f32[8,1024]{1,0:T(8,128)}, f32[32,128]{1,0:T(8,128)}) custom-call(s32[1,1,8]{2,1,0:T(1,128)} %count_from.1, f32[1,1,8,1024]{3,2,1,0:T(8,128)} %weight_from.1, f32[1,1,8,1024]{3,2,1,0:T(8,128)} %magnitude_from.1, s32[1,1,8,1024]{3,2,1,0:T(8,128)} %star_ref.3), custom_call_target="tpu_custom_call" | custom-call | flops 2000000000 | bytes 1048576 | tf_op jit(solution)/shard_map/pallas_call | solution.py:335
  3.3 0.0 copy-start
  3.3 7.3 %all-to-all-start = ((f32[32,8,128]{2,1,0:T(8,128)}), f32[32,8,128]{2,1,0:T(8,128)S(1)}, u32[]{:S(2)}, u32[]{:S(2)}) async-start(f32[32,8,128]{2,1,0:T(8,128)} %get-tuple-element.15), calls=%async_computation | async-start | bytes 262144 | tf_op jit(solution)/shard_map/all_to_all | solution.py:327
  10.6 0.0 copy-done
  10.7 2.7 %collective-permute-start.2 = (s32[1,1,8,1024]{3,2,1,0:T(8,128)S(1)}, s32[1,1,8,1024]{3,2,1,0:T(8,128)S(1)}, u32[]{:S(2)}, u32[]{:S(2)}) collective-permute-start(s32[1,1,8,1024]{3,2,1,0:T(8,128)S(1)} %copy-done), channel_id=1, source_target_pairs={{0,24},{8,16},{16,8},{24,0},{1,25},{9,17},{17,9},{25,1},{2,26},{10... | collective-permute-start | bytes 98312 | tf_op jit(solution)/shard_map/ppermute | solution.py:332
  13.4 0.6 collective-permute-start.1
  13.9 0.3 collective-permute-start
  14.2 4.6 %all-to-all-done.arrived_ref = f32[32,8,128]{2,1,0:T(8,128)S(1)} async-done(((f32[32,8,128]{2,1,0:T(8,128)}), f32[32,8,128]{2,1,0:T(8,128)S(1)}, u32[]{:S(2)}, u32[]{:S(2)}) %all-to-all-start) | async-done | bytes 131104 | tf_op jit(solution)/shard_map/all_to_all | solution.py:327
  18.8 0.8 %shard_map.69.part_ref = f32[96,128]{1,0:T(8,128)S(1)} custom-call(s32[1]{0:T(128)} %bitcast.me_ref, f32[32,8,128]{2,1,0:T(8,128)S(1)} %all-to-all-done.arrived_ref, s32[1,1,8,1024]{3,2,1,0:T(8,128)S(1)} %copy-done), custom_call_target="tpu_custom_call" | custom-call | flops 2000000000 | bytes 1048576 | tf_op jit(solution)/shard_map/pallas_call | solution.py:345
  19.6 0.0 collective-permute-done.2.refs_3_
  19.6 0.0 collective-permute-done.1.refs_2_
  19.6 0.0 collective-permute-done.refs_1_
  19.7 0.0 copy-start.3
  19.7 3.0 %shard_map.70 = (f32[64,128]{1,0:T(8,128)S(1)}, s32[32,1024]{1,0:T(8,128)S(1)}, f32[96,128]{1,0:T(8,128)S(1)}) custom-call(s32[1]{0:T(128)} %bitcast.me_ref, f32[32,8,128]{2,1,0:T(8,128)S(1)} %all-to-all-done.arrived_ref, f32[96,128]{1,0:T(8,128)S(1)} %shard_map.69.part_ref, s32[1,1,8,1024]{3,2,1,0:T(8,128)S(1)} %copy-done, ...), custom_call_target="tpu_custom_call" | custom-call | tf_op jit(solution)/shard_map/pallas_call | solution.py:346
  22.6 0.0 copy-start.1
  22.7 0.0 copy-start.2
  22.7 8.3 %all_to_all.37.values_ref.first_ref = f32[8,8,128]{2,1,0:T(8,128)S(1)} all-to-all(f32[8,8,128]{2,1,0:T(8,128)S(1)} %bitcast.18), channel_id=1, replica_groups=mesh['sky'=4,'exp'=8] {'exp'}, dimensions={0} | all-to-all | bytes 65536 | tf_op jit(solution)/shard_map/all_to_all | solution.py:330
  31.0 0.0 copy-done.3
  31.0 0.0 copy-done.1
  31.0 0.0 copy-done.2
  31.0 1.1 %shard_map.71 = f32[32,8,128]{2,1,0:T(8,128)S(1)} custom-call(f32[8,8,128]{2,1,0:T(8,128)S(1)} %all_to_all.37.values_ref.first_ref, s32[1,1,8,1024]{3,2,1,0:T(8,128)S(1)} %copy-done.1, f32[8,1024]{1,0:T(8,128)S(1)} %copy-done.2, f32[32,128]{1,0:T(8,128)S(1)} %copy-done.3), custom_call_target="tpu_custom_call" | custom-call | flops 2000000000 | bytes 1048576 | tf_op jit(solution)/shard_map/pallas_call | solution.py:354
  32.1 9.9 %all_to_all.38.arrived_ref = f32[32,8,128]{2,1,0:T(8,128)S(1)} all-to-all(f32[32,8,128]{2,1,0:T(8,128)S(1)} %shard_map.71), channel_id=1, replica_groups=mesh['sky'=4,'exp'=8] {'sky','exp'}, dimensions={0} | all-to-all | bytes 262144 | tf_op jit(solution)/shard_map/all_to_all | solution.py:327
  42.1 3.6 %shard_map.72 = (f32[72,128]{1,0:T(8,128)S(1)}, f32[96,128]{1,0:T(8,128)S(1)}) custom-call(f32[32,8,128]{2,1,0:T(8,128)S(1)} %all_to_all.38.arrived_ref, s32[32,1024]{1,0:T(8,128)S(1)} %get-tuple-element.19.all_ref, f32[96,128]{1,0:T(8,128)S(1)} %get-tuple-element.20.right_ref, s32[1,1,8,1024]{3,2,1,0:T(8,128)S(1)} %copy-done), custom_call_target="tpu_custom_call" | custom-call | flops 2000000000 | bytes 1048576 | tf_op jit(solution)/shard_map/pallas_call | solution.py:356
  45.7 8.1 %all_to_all.39 = f32[8,1,1152]{2,1,0:T(1,128)S(1)} all-to-all(f32[8,1,1152]{2,1,0:T(1,128)S(1)} %bitcast.17), channel_id=1, replica_groups=mesh['sky'=4,'exp'=8] {'exp'}, dimensions={0} | all-to-all | bytes 73728 | tf_op jit(solution)/shard_map/all_to_all | solution.py:330
  53.8 1.3 %shard_map.73 = (f32[288,128]{1,0:T(8,128)S(1)}, f32[96,128]{1,0:T(8,128)S(1)}, f32[8,128]{1,0:T(8,128)S(1)}) custom-call(f32[8,8,128]{2,1,0:T(8,128)S(1)} %all_to_all.37.values_ref.first_ref, f32[8,1152]{1,0:T(8,128)S(1)} %bitcast.16, s32[1,1,8,1024]{3,2,1,0:T(8,128)S(1)} %copy-done.1, f32[8,1024]{1,0:T(8,128)S(1)} %copy-done.2, f32[32,128]{1,0:T(8,128)S(1)} %copy-done.3, ...), custom_call_target="tpu_custom_call" | custom-call | flops 2000000000 | bytes 1048576 | tf_op jit(solution)/shard_map/pallas_call | solution.py:358
  55.2 10.0 %all_to_all.40 = f32[32,1,1152]{2,1,0:T(1,128)S(1)} all-to-all(f32[32,1,1152]{2,1,0:T(1,128)S(1)} %bitcast.15), channel_id=1, replica_groups=mesh['sky'=4,'exp'=8] {'sky','exp'}, dimensions={0} | all-to-all | bytes 294912 | tf_op jit(solution)/shard_map/all_to_all | solution.py:327
  65.2 3.5 %shard_map.74 = (f32[96,128]{1,0:T(8,128)}, f32[96,128]{1,0:T(8,128)}) custom-call(f32[32,1152]{1,0:T(8,128)S(1)} %bitcast.14, s32[32,1024]{1,0:T(8,128)S(1)} %get-tuple-element.19.all_ref, f32[96,128]{1,0:T(8,128)S(1)} %get-tuple-element.20.right_ref, f32[96,128]{1,0:T(8,128)S(1)} %get-tuple-element.22.image_ref, ...), custom_call_target="tpu_custom_call" | custom-call | flops 2000000000 | bytes 1048576 | tf_op jit(solution)/shard_map/pallas_call | solution.py:362
  (2 shorter events, 0.0 us)
Async XLA Ops:
  3.3 7.3 %copy-start = (s32[1,1,8,1024]{3,2,1,0:T(8,128)S(1)}, s32[1,1,8,1024]{3,2,1,0:T(8,128)}, u32[]{:S(2)}) copy-start(s32[1,1,8,1024]{3,2,1,0:T(8,128)} %zp_ref.3) | copy-start | bytes 98308
  3.3 15.5 %all-to-all-start = ((f32[32,8,128]{2,1,0:T(8,128)}), f32[32,8,128]{2,1,0:T(8,128)S(1)}, u32[]{:S(2)}, u32[]{:S(2)}) async-start(f32[32,8,128]{2,1,0:T(8,128)} %get-tuple-element.15), calls=%async_computation | async-start | bytes 262144 | tf_op jit(solution)/shard_map/all_to_all | solution.py:327
  10.7 9.0 %collective-permute-start.2 = (s32[1,1,8,1024]{3,2,1,0:T(8,128)S(1)}, s32[1,1,8,1024]{3,2,1,0:T(8,128)S(1)}, u32[]{:S(2)}, u32[]{:S(2)}) collective-permute-start(s32[1,1,8,1024]{3,2,1,0:T(8,128)S(1)} %copy-done), channel_id=1, source_target_pairs={{0,24},{8,16},{16,8},{24,0},{1,25},{9,17},{17,9},{25,1},{2,26},{10... | collective-permute-start | bytes 98312 | tf_op jit(solution)/shard_map/ppermute | solution.py:332
  13.4 6.3 %collective-permute-start.1 = (s32[1,1,8,1024]{3,2,1,0:T(8,128)S(1)}, s32[1,1,8,1024]{3,2,1,0:T(8,128)S(1)}, u32[]{:S(2)}, u32[]{:S(2)}) collective-permute-start(s32[1,1,8,1024]{3,2,1,0:T(8,128)S(1)} %copy-done), channel_id=1, source_target_pairs={{0,16},{8,24},{16,0},{24,8},{1,17},{9,25},{17,1},{25,9},{2,18},{10... | collective-permute-start | bytes 98312 | tf_op jit(solution)/shard_map/ppermute | solution.py:332
  13.9 5.7 %collective-permute-start = (s32[1,1,8,1024]{3,2,1,0:T(8,128)S(1)}, s32[1,1,8,1024]{3,2,1,0:T(8,128)S(1)}, u32[]{:S(2)}, u32[]{:S(2)}) collective-permute-start(s32[1,1,8,1024]{3,2,1,0:T(8,128)S(1)} %copy-done), channel_id=1, source_target_pairs={{0,8},{8,0},{16,24},{24,16},{1,9},{9,1},{17,25},{25,17},{2,10},{10... | collective-permute-start | bytes 98312 | tf_op jit(solution)/shard_map/ppermute | solution.py:332
  19.7 11.3 %copy-start.3 = (f32[32,128]{1,0:T(8,128)S(1)}, f32[32,128]{1,0:T(8,128)}, u32[]{:S(2)}) copy-start(f32[32,128]{1,0:T(8,128)} %get-tuple-element.18.scale_ref) | copy-start | bytes 49156
  22.6 8.4 %copy-start.1 = (s32[1,1,8,1024]{3,2,1,0:T(8,128)S(1)}, s32[1,1,8,1024]{3,2,1,0:T(8,128)}, u32[]{:S(2)}) copy-start(s32[1,1,8,1024]{3,2,1,0:T(8,128)} %star_ref.3) | copy-start | bytes 98308
  22.7 8.4 %copy-start.2 = (f32[8,1024]{1,0:T(8,128)S(1)}, f32[8,1024]{1,0:T(8,128)}, u32[]{:S(2)}) copy-start(f32[8,1024]{1,0:T(8,128)} %get-tuple-element.17.live_ref) | copy-start | bytes 98308

commit v7 on v6

--- a/solution.py
+++ b/solution.py
@@ -341,6 +341,7 @@
         compiler_params=pltpu.CompilerParams(vmem_limit_bytes=58 << 20),
         cost_estimate=pl.CostEstimate(flops=2_000_000_000, bytes_accessed=1 << 20, transcendentals=0),
     )(peer_count, obs_weight, magnitude, star_id)
+    sent, zp[1] = lax.optimization_barrier((sent, zp[1]))
     arrived = to_owners(sent)
     (part,) = call(own_owner, [tall], in_specs=[smem, vmem, vmem])(me, arrived, zp_index)
     sent, zp_all, right = pl.pallas_call(

time: 69.1 us -> 70.4 us (1.019)
  starting transfers between devices: 10.9 us -> 12.1 us
    ppermute x3, starting transfers between devices: 3.55 us -> 6.3 us  [body(): lax.ppermute(zp_index, 'sky', [(i, i ^ d) for i in range(n_sky)])]
    all_to_all x1, starting transfers between devices: 7.31 us -> 5.78 us  [to_owners(): lax.all_to_all(x, ('sky', 'exp'), split_axis=0, concat_axis=0, tiled=True)]
  transfers between devices with their start and end apart: 4 -> 4, of which waited for: 1 -> 1; matrix products, arithmetic and copies ran while one was open for 0% -> 0% of each run, Pallas kernels for 1% -> 5%
where the time goes in v7:
time: 70.4 us; the launch traced here: 69.9 us
  blocking collectives  36.1 us (51%)
  Pallas kernels  16 us (23%)
  starting transfers between devices  12.1 us (17%)
  waiting for transfers between devices  4.88 us (7%)
  between operations  0.75 us (1%)
    all_to_all x2, blocking collectives, to_owners(): lax.all_to_all(x, ('sky', 'exp'), split_axis=0, concat_axis=0, tiled=True)  19.9 us
    all_to_all x2, blocking collectives, to_sources(): return lax.all_to_all(x, 'exp', split_axis=0, concat_axis=0, tiled=True)  16.3 us
    ppermute x3, starting transfers between devices, body(): lax.ppermute(zp_index, 'sky', [(i, i ^ d) for i in range(n_sky)])  6.3 us
    all_to_all x1, starting transfers between devices, to_owners(): lax.all_to_all(x, ('sky', 'exp'), split_axis=0, concat_axis=0, tiled=True)  5.78 us
    all_to_all x1, waiting for transfers between devices, to_owners(): lax.all_to_all(x, ('sky', 'exp'), split_axis=0, concat_axis=0, tiled=True)  4.87 us
    pallas_call x1, Pallas kernels, body(): call(second_owner, [picks, tall])(arrived, zp_all, right, zp_index)  3.63 us
    pallas_call x1, Pallas kernels, body(): call(last_owner, [tall, tall], [tall])  3.51 us
    pallas_call x1, Pallas kernels, body(): pl.pallas_call(functools.partial(first_owner, n_sky), out_shape=[jax.Shap...  2.96 us
  transfers between devices with their start and end apart: 4, of which 1 were waited for; matrix products, arithmetic and copies ran while one was open for 0% of the time, Pallas kernels for 5%

profile of v7, /device:TPU:0, one launch (start us, length us, event | category | flops | bytes accessed | tf_op | source)
XLA Modules:
  0.0 69.9 jit_solution(1718550093510399244)
XLA Ops:
  0.6 3.0 %collective-permute-start = (s32[1,1,8,1024]{3,2,1,0:T(8,128)}, s32[1,1,8,1024]{3,2,1,0:T(8,128)S(1)}, u32[]{:S(2)}, u32[]{:S(2)}) collective-permute-start(s32[1,1,8,1024]{3,2,1,0:T(8,128)} %zp_ref.3), channel_id=1, source_target_pairs={{0,8},{8,0},{16,24},{24,16},{1,9},{9,1},{17,25},{25,17},{2,10},{10... | collective-permute-start | bytes 98312 | tf_op jit(solution)/shard_map/ppermute | solution.py:332
  3.6 2.7 %shard_map.68 = (f32[32,8,128]{2,1,0:T(8,128)}, f32[8,1024]{1,0:T(8,128)}, f32[32,128]{1,0:T(8,128)}) custom-call(s32[1,1,8]{2,1,0:T(1,128)} %count_from.1, f32[1,1,8,1024]{3,2,1,0:T(8,128)} %weight_from.1, f32[1,1,8,1024]{3,2,1,0:T(8,128)} %magnitude_from.1, s32[1,1,8,1024]{3,2,1,0:T(8,128)} %star_ref.3), custom_call_target="tpu_custom_call" | custom-call | flops 2000000000 | bytes 1048576 | tf_op jit(solution)/shard_map/pallas_call | solution.py:335
  6.3 0.0 collective-permute-done.refs_1_
  6.3 0.0 copy-start
  6.3 5.8 %all-to-all-start = ((f32[32,8,128]{2,1,0:T(8,128)}), f32[32,8,128]{2,1,0:T(8,128)S(1)}, u32[]{:S(2)}, u32[]{:S(2)}) async-start(f32[32,8,128]{2,1,0:T(8,128)} %get-tuple-element.18), calls=%async_computation | async-start | bytes 262144 | tf_op jit(solution)/shard_map/all_to_all | solution.py:327
  12.1 0.0 copy-done
  12.1 2.7 %collective-permute-start.2 = (s32[1,1,8,1024]{3,2,1,0:T(8,128)S(1)}, s32[1,1,8,1024]{3,2,1,0:T(8,128)S(1)}, u32[]{:S(2)}, u32[]{:S(2)}) collective-permute-start(s32[1,1,8,1024]{3,2,1,0:T(8,128)S(1)} %copy-done), channel_id=1, source_target_pairs={{0,24},{8,16},{16,8},{24,0},{1,25},{9,17},{17,9},{25,1},{2,26},{10... | collective-permute-start | bytes 98312 | tf_op jit(solution)/shard_map/ppermute | solution.py:332
  14.9 0.6 collective-permute-start.1
  15.4 4.9 %all-to-all-done.arrived_ref = f32[32,8,128]{2,1,0:T(8,128)S(1)} async-done(((f32[32,8,128]{2,1,0:T(8,128)}), f32[32,8,128]{2,1,0:T(8,128)S(1)}, u32[]{:S(2)}, u32[]{:S(2)}) %all-to-all-start) | async-done | bytes 131104 | tf_op jit(solution)/shard_map/all_to_all | solution.py:327
  20.3 0.8 %shard_map.69.part_ref = f32[96,128]{1,0:T(8,128)S(1)} custom-call(s32[1]{0:T(128)} %bitcast.me_ref, f32[32,8,128]{2,1,0:T(8,128)S(1)} %all-to-all-done.arrived_ref, s32[1,1,8,1024]{3,2,1,0:T(8,128)S(1)} %copy-done), custom_call_target="tpu_custom_call" | custom-call | flops 2000000000 | bytes 1048576 | tf_op jit(solution)/shard_map/pallas_call | solution.py:346
  21.1 0.0 collective-permute-done.2.refs_3_
  21.1 0.0 collective-permute-done.1.refs_2_
  21.1 0.0 copy-start.3
  21.1 3.0 %shard_map.70 = (f32[64,128]{1,0:T(8,128)S(1)}, s32[32,1024]{1,0:T(8,128)S(1)}, f32[96,128]{1,0:T(8,128)S(1)}) custom-call(s32[1]{0:T(128)} %bitcast.me_ref, f32[32,8,128]{2,1,0:T(8,128)S(1)} %all-to-all-done.arrived_ref, f32[96,128]{1,0:T(8,128)S(1)} %shard_map.69.part_ref, s32[1,1,8,1024]{3,2,1,0:T(8,128)S(1)} %copy-done, ...), custom_call_target="tpu_custom_call" | custom-call | tf_op jit(solution)/shard_map/pallas_call | solution.py:347
  24.1 0.0 copy-start.1
  24.1 0.0 copy-start.2
  24.1 8.1 %all_to_all.37.values_ref.first_ref = f32[8,8,128]{2,1,0:T(8,128)S(1)} all-to-all(f32[8,8,128]{2,1,0:T(8,128)S(1)} %bitcast.18), channel_id=1, replica_groups=mesh['sky'=4,'exp'=8] {'exp'}, dimensions={0} | all-to-all | bytes 65536 | tf_op jit(solution)/shard_map/all_to_all | solution.py:330
  32.3 0.0 copy-done.3
  32.3 0.0 copy-done.1
  32.3 0.0 copy-done.2
  32.3 1.1 %shard_map.71 = f32[32,8,128]{2,1,0:T(8,128)S(1)} custom-call(f32[8,8,128]{2,1,0:T(8,128)S(1)} %all_to_all.37.values_ref.first_ref, s32[1,1,8,1024]{3,2,1,0:T(8,128)S(1)} %copy-done.1, f32[8,1024]{1,0:T(8,128)S(1)} %copy-done.2, f32[32,128]{1,0:T(8,128)S(1)} %copy-done.3), custom_call_target="tpu_custom_call" | custom-call | flops 2000000000 | bytes 1048576 | tf_op jit(solution)/shard_map/pallas_call | solution.py:355
  33.4 9.9 %all_to_all.38.arrived_ref = f32[32,8,128]{2,1,0:T(8,128)S(1)} all-to-all(f32[32,8,128]{2,1,0:T(8,128)S(1)} %shard_map.71), channel_id=1, replica_groups=mesh['sky'=4,'exp'=8] {'sky','exp'}, dimensions={0} | all-to-all | bytes 262144 | tf_op jit(solution)/shard_map/all_to_all | solution.py:327
  43.3 3.6 %shard_map.72 = (f32[72,128]{1,0:T(8,128)S(1)}, f32[96,128]{1,0:T(8,128)S(1)}) custom-call(f32[32,8,128]{2,1,0:T(8,128)S(1)} %all_to_all.38.arrived_ref, s32[32,1024]{1,0:T(8,128)S(1)} %get-tuple-element.23.all_ref, f32[96,128]{1,0:T(8,128)S(1)} %get-tuple-element.24.right_ref, s32[1,1,8,1024]{3,2,1,0:T(8,128)S(1)} %copy-done), custom_call_target="tpu_custom_call" | custom-call | flops 2000000000 | bytes 1048576 | tf_op jit(solution)/shard_map/pallas_call | solution.py:357
  46.9 8.1 %all_to_all.39 = f32[8,1,1152]{2,1,0:T(1,128)S(1)} all-to-all(f32[8,1,1152]{2,1,0:T(1,128)S(1)} %bitcast.17), channel_id=1, replica_groups=mesh['sky'=4,'exp'=8] {'exp'}, dimensions={0} | all-to-all | bytes 73728 | tf_op jit(solution)/shard_map/all_to_all | solution.py:330
  55.0 1.3 %shard_map.73 = (f32[288,128]{1,0:T(8,128)S(1)}, f32[96,128]{1,0:T(8,128)S(1)}, f32[8,128]{1,0:T(8,128)S(1)}) custom-call(f32[8,8,128]{2,1,0:T(8,128)S(1)} %all_to_all.37.values_ref.first_ref, f32[8,1152]{1,0:T(8,128)S(1)} %bitcast.16, s32[1,1,8,1024]{3,2,1,0:T(8,128)S(1)} %copy-done.1, f32[8,1024]{1,0:T(8,128)S(1)} %copy-done.2, f32[32,128]{1,0:T(8,128)S(1)} %copy-done.3, ...), custom_call_target="tpu_custom_call" | custom-call | flops 2000000000 | bytes 1048576 | tf_op jit(solution)/shard_map/pallas_call | solution.py:359
  56.4 10.0 %all_to_all.40 = f32[32,1,1152]{2,1,0:T(1,128)S(1)} all-to-all(f32[32,1,1152]{2,1,0:T(1,128)S(1)} %bitcast.15), channel_id=1, replica_groups=mesh['sky'=4,'exp'=8] {'sky','exp'}, dimensions={0} | all-to-all | bytes 294912 | tf_op jit(solution)/shard_map/all_to_all | solution.py:327
  66.4 3.5 %shard_map.74 = (f32[96,128]{1,0:T(8,128)}, f32[96,128]{1,0:T(8,128)}) custom-call(f32[32,1152]{1,0:T(8,128)S(1)} %bitcast.14, s32[32,1024]{1,0:T(8,128)S(1)} %get-tuple-element.23.all_ref, f32[96,128]{1,0:T(8,128)S(1)} %get-tuple-element.24.right_ref, f32[96,128]{1,0:T(8,128)S(1)} %get-tuple-element.26.image_ref, ...), custom_call_target="tpu_custom_call" | custom-call | flops 2000000000 | bytes 1048576 | tf_op jit(solution)/shard_map/pallas_call | solution.py:363
  (2 shorter events, 0.0 us)
Async XLA Ops:
  0.6 5.7 %collective-permute-start = (s32[1,1,8,1024]{3,2,1,0:T(8,128)}, s32[1,1,8,1024]{3,2,1,0:T(8,128)S(1)}, u32[]{:S(2)}, u32[]{:S(2)}) collective-permute-start(s32[1,1,8,1024]{3,2,1,0:T(8,128)} %zp_ref.3), channel_id=1, source_target_pairs={{0,8},{8,0},{16,24},{24,16},{1,9},{9,1},{17,25},{25,17},{2,10},{10... | collective-permute-start | bytes 98312 | tf_op jit(solution)/shard_map/ppermute | solution.py:332
  6.3 5.8 %copy-start = (s32[1,1,8,1024]{3,2,1,0:T(8,128)S(1)}, s32[1,1,8,1024]{3,2,1,0:T(8,128)}, u32[]{:S(2)}) copy-start(s32[1,1,8,1024]{3,2,1,0:T(8,128)} %zp_ref.3) | copy-start | bytes 98308
  6.3 14.0 %all-to-all-start = ((f32[32,8,128]{2,1,0:T(8,128)}), f32[32,8,128]{2,1,0:T(8,128)S(1)}, u32[]{:S(2)}, u32[]{:S(2)}) async-start(f32[32,8,128]{2,1,0:T(8,128)} %get-tuple-element.18), calls=%async_computation | async-start | bytes 262144 | tf_op jit(solution)/shard_map/all_to_all | solution.py:327
  12.1 9.0 %collective-permute-start.2 = (s32[1,1,8,1024]{3,2,1,0:T(8,128)S(1)}, s32[1,1,8,1024]{3,2,1,0:T(8,128)S(1)}, u32[]{:S(2)}, u32[]{:S(2)}) collective-permute-start(s32[1,1,8,1024]{3,2,1,0:T(8,128)S(1)} %copy-done), channel_id=1, source_target_pairs={{0,24},{8,16},{16,8},{24,0},{1,25},{9,17},{17,9},{25,1},{2,26},{10... | collective-permute-start | bytes 98312 | tf_op jit(solution)/shard_map/ppermute | solution.py:332
  14.9 6.3 %collective-permute-start.1 = (s32[1,1,8,1024]{3,2,1,0:T(8,128)S(1)}, s32[1,1,8,1024]{3,2,1,0:T(8,128)S(1)}, u32[]{:S(2)}, u32[]{:S(2)}) collective-permute-start(s32[1,1,8,1024]{3,2,1,0:T(8,128)S(1)} %copy-done), channel_id=1, source_target_pairs={{0,16},{8,24},{16,0},{24,8},{1,17},{9,25},{17,1},{25,9},{2,18},{10... | collective-permute-start | bytes 98312 | tf_op jit(solution)/shard_map/ppermute | solution.py:332
  21.1 11.1 %copy-start.3 = (f32[32,128]{1,0:T(8,128)S(1)}, f32[32,128]{1,0:T(8,128)}, u32[]{:S(2)}) copy-start(f32[32,128]{1,0:T(8,128)} %get-tuple-element.22.scale_ref) | copy-start | bytes 49156
  24.1 8.1 %copy-start.1 = (s32[1,1,8,1024]{3,2,1,0:T(8,128)S(1)}, s32[1,1,8,1024]{3,2,1,0:T(8,128)}, u32[]{:S(2)}) copy-start(s32[1,1,8,1024]{3,2,1,0:T(8,128)} %star_ref.3) | copy-start | bytes 98308
  24.1 8.1 %copy-start.2 = (f32[8,1024]{1,0:T(8,128)S(1)}, f32[8,1024]{1,0:T(8,128)}, u32[]{:S(2)}) copy-start(f32[8,1024]{1,0:T(8,128)} %get-tuple-element.21.live_ref) | copy-start | bytes 98308
